TPU v7x, 32 devices: a whole 2x2x4 slice. The times are simulated.
32 devices in a mesh: req: 8 (over z, y), tp: 4 (over x, core).
Axes of the slice: x: 2, y: 2, z: 4, core: 2. Of those that a mesh axis runs over, the one named last changes fastest.
Arguments:
- ssm_input: bfloat16 [8, 512, 8192], P('req', 'tp'), may hold values from -6 to 6
- ssm_gate: bfloat16 [8, 512, 8192], P('req', 'tp'), may hold values from -6 to 6
- state_proj: bfloat16 [8, 512, 4096], P('req', 'tp'), may hold values from -1.796875 to 1.796875
- step_raw: bfloat16 [8, 512, 128], P('req', 'tp'), may hold values from -3 to 3
- queries: bfloat16 [8, 512, 4096], P('req', 'tp'), may hold values from -5 to 5
- fresh_kv: bfloat16 [8, 512, 2048], P('req', 'tp'), may hold values from -6 to 6
- block_pool: bfloat16 [32, 64, 8, 256], P('req', None, 'tp'), may hold values from -5 to 5
- state_pool: bfloat16 [8, 128, 64, 256], P('req', 'tp'), may hold values from -16 to 16
- decay_log: float32 [128], P('tp'), may hold values from -10 to -1
- step_bias: float32 [128], P('tp'), may hold values from -1 to 0
- skip_gain: float32 [128], P('tp'), may hold values from 1 to 3
- norm_gain: float32 [8192], P('tp'), may hold values from 0.5 to 1.5
- block_owner: int32 [8, 64], replicated, may hold values from 0 to 7, as said below
- block_slot: int32 [8, 64], replicated, may hold values from 0 to 3, as said below
- block_count: int32 [8], replicated, may hold values from 32 to 64, as said below
- state_entry: int32 [8], replicated, may hold values from 0 to 7
- suffix_len: int32 [8], replicated, may hold values from 128 to 512, as said below
Outputs:
- ssm_out: bfloat16 [8, 512, 8192], P('req', 'tp')
- attn_out: bfloat16 [8, 512, 4096], P('req', 'tp')
Inputs may be any that keep to these rules, and one draw needn't show every extreme that they name: `block_owner`: among the first block_count[r] entries of a request no owner appears more than 8 times; in every draw one request has 64 entries in use and takes exactly 8 from every owner. The owner at entry j is named again at entry j + 8. Requests 4k to 4k + 3 name the same owners at every entry. `block_slot`: requests 4k to 4k + 3 name the same blocks in their first 32 entries. `block_count`: some request has 64 in every draw. `suffix_len`: some request has 512 in every draw.
All inputs are finite; a program needn't handle non-finite values.
Results may differ from a plain program's by a relative error of at most 0.0048.
Values may be sent and summed in bfloat16 or wider, within the bound.
No kernel may reach another device: no remote copies, remote signals or barrier semaphores. Data moves between devices by JAX's collectives and lax.ppermute only.
A program may use at most 128 MiB of HBM per device.

v0:
```python
import jax
import jax.numpy as jnp
from jax import lax
from jax.sharding import PartitionSpec as P

STATE = 256
SPAN = 256


def scan_heads(
    ssm_rows,
    gate_rows,
    proj_rows,
    step_rows,
    initial,
    decay_log,
    step_bias,
    skip_gain,
    norm_gain,
    live_len,
    group_count,
):
    length_all, width = ssm_rows.shape
    head_count = step_rows.shape[1]
    head_size = width // head_count
    per_group = head_count // group_count
    state_size = proj_rows.shape[1] // (2 * group_count)
    block_count = length_all // SPAN
    inputs = ssm_rows.reshape(block_count, SPAN, group_count, per_group, head_size)
    proj_four = proj_rows.reshape(block_count, SPAN, group_count, 2, state_size)
    in_proj = proj_four[:, :, :, 0]
    out_proj = proj_four[:, :, :, 1]
    step_size = jax.nn.softplus(step_rows.astype(jnp.float32) + step_bias[None, :])
    step_size = step_size.reshape(block_count, SPAN, group_count, per_group)
    rates = jnp.exp(decay_log).reshape(group_count, per_group)
    skip_heads = skip_gain.reshape(group_count, per_group)
    lower = jnp.arange(SPAN)[:, None] >= jnp.arange(SPAN)[None, :]

    def advance(state, block_in):
        block_x, block_b, block_c, block_dt = block_in
        cumul = jnp.cumsum(-rates[None] * block_dt, axis=0)
        inner = jnp.einsum("tgn,ugn->tug", block_c, block_b, preferred_element_type=jnp.float32)
        spread = cumul[:, None] - cumul[None, :]
        decay = jnp.exp(jnp.where(lower[:, :, None, None], spread, -jnp.inf))
        mixing = (decay * inner[:, :, :, None] * block_dt[None]).astype(jnp.bfloat16)
        output = jnp.einsum("tugh,ughp->tghp", mixing, block_x, preferred_element_type=jnp.float32)
        state_in = state.astype(jnp.bfloat16)
        carried = jnp.einsum(
            "tgn,ghpn->tghp", block_c, state_in, preferred_element_type=jnp.float32
        )
        output = output + jnp.exp(cumul)[..., None] * carried
        output = output + skip_heads[None, :, :, None] * block_x.astype(jnp.float32)
        tail_weight = jnp.exp(cumul[-1][None] - cumul) * block_dt
        tail_terms = (tail_weight[..., None] * block_x).astype(jnp.bfloat16)
        state = jnp.exp(cumul[-1])[:, :, None, None] * state + jnp.einsum(
            "ughp,ugn->ghpn", tail_terms, block_b, preferred_element_type=jnp.float32
        )
        return (state, output)

    start_state = initial.reshape(group_count, per_group, head_size, state_size)
    final_state, outputs = lax.scan(advance, start_state, (inputs, in_proj, out_proj, step_size))
    outputs = outputs.reshape(length_all, group_count, per_group * head_size)
    gated = outputs * jax.nn.silu(gate_rows.astype(jnp.float32)).reshape(
        length_all, group_count, per_group * head_size
    )
    mean_sq = jnp.mean(gated * gated, axis=-1, keepdims=True)
    normed = (
        gated * lax.rsqrt(mean_sq + 1e-05) * norm_gain.reshape(group_count, per_group * head_size)
    )
    normed = normed.reshape(length_all, width)
    alive = jnp.arange(length_all) < live_len
    return jnp.where(alive[:, None], normed, 0.0).astype(jnp.bfloat16)


def attend(query_rows, key_rows, value_rows, prefix_live, live_len):
    length_all, kv_count, repeat, head_size = query_rows.shape
    key_total = key_rows.shape[0]
    prefix_rows = key_total - length_all
    rows_block = min(256, length_all)
    inv_root = 1.0 / head_size**0.5
    key_index = jnp.arange(key_total)

    def one_block(offset):
        block_q = lax.dynamic_slice_in_dim(query_rows, offset, rows_block, 0)
        scores = (
            jnp.einsum("qcrd,kcd->crqk", block_q, key_rows, preferred_element_type=jnp.float32)
            * inv_root
        )
        query_index = offset + jnp.arange(rows_block)
        allowed = jnp.where(
            key_index[None, :] < prefix_rows,
            key_index[None, :] < prefix_live,
            key_index[None, :] - prefix_rows <= query_index[:, None],
        )
        scores = jnp.where(allowed[None, None], scores, -jnp.inf)
        row_max = jnp.max(scores, axis=-1, keepdims=True)
        expon = jnp.exp(scores - row_max)
        totals = jnp.sum(expon, axis=-1)
        weights = expon.astype(jnp.bfloat16)
        mixed = jnp.einsum(
            "crqk,kcd->qcrd", weights, value_rows, preferred_element_type=jnp.float32
        )
        mixed = mixed / jnp.transpose(totals, (2, 0, 1))[..., None]
        mixed = jnp.where((query_index < live_len)[:, None, None, None], mixed, 0.0)
        return mixed.astype(jnp.bfloat16)

    outputs = lax.map(one_block, jnp.arange(length_all // rows_block, dtype=jnp.int32) * rows_block)
    return outputs.reshape(length_all, kv_count * repeat * head_size)


def per_device(
    ssm_input,
    ssm_gate,
    state_proj,
    step_raw,
    queries,
    fresh_kv,
    block_pool,
    state_pool,
    decay_log,
    step_bias,
    skip_gain,
    norm_gain,
    block_owner,
    block_slot,
    block_count,
    state_entry,
    suffix_len,
):
    my_index = lax.axis_index("req")
    ssm_rows, gate_rows, proj_rows, step_rows, query_rows, fresh_rows = (
        lax.all_to_all(ssm_input, "tp", split_axis=2, concat_axis=1, tiled=True),
        lax.all_to_all(ssm_gate, "tp", split_axis=2, concat_axis=1, tiled=True),
        lax.all_to_all(state_proj, "tp", split_axis=2, concat_axis=1, tiled=True),
        lax.all_to_all(step_raw, "tp", split_axis=2, concat_axis=1, tiled=True),
        lax.all_to_all(queries, "tp", split_axis=2, concat_axis=1, tiled=True),
        lax.all_to_all(fresh_kv, "tp", split_axis=2, concat_axis=1, tiled=True),
    )
    wanted = state_entry[my_index]
    shard_rows = lax.all_gather(state_pool, "req", axis=0, tiled=True)
    marks = (jnp.arange(shard_rows.shape[0]) == wanted).astype(jnp.bfloat16)
    initial = jnp.einsum("e,emdn->mdn", marks, shard_rows, preferred_element_type=jnp.float32)
    live_len = suffix_len[my_index]
    local_groups = state_proj.shape[2] // (2 * STATE) // lax.axis_size("tp")
    mamba = scan_heads(
        ssm_rows[0],
        gate_rows[0],
        proj_rows[0],
        step_rows[0],
        initial,
        decay_log,
        step_bias,
        skip_gain,
        norm_gain,
        live_len,
        local_groups,
    )
    owners_row = block_owner[my_index]
    slots_row = block_slot[my_index]
    pool_local = block_pool.shape[0]
    table_len = block_owner.shape[1]
    targets = owners_row * pool_local + slots_row
    blank_blocks = jnp.zeros((table_len,) + block_pool.shape[1:], jnp.bfloat16)
    shard_rows = lax.all_gather(block_pool, "req", axis=0, tiled=True)
    inside = (targets >= 0) & (targets < shard_rows.shape[0])
    taken = shard_rows[jnp.clip(targets, 0, shard_rows.shape[0] - 1)]
    fetched = jnp.where(inside[:, None, None, None], taken, blank_blocks)
    kv_local = block_pool.shape[2]
    head_size = block_pool.shape[3] // 2
    length_all = ssm_rows.shape[1]
    cached = fetched.reshape(table_len * block_pool.shape[1], kv_local, 2 * head_size)
    newest = fresh_rows[0].reshape(length_all, kv_local, 2 * head_size)
    joined = jnp.concatenate([cached, newest], axis=0)
    grouped_q = query_rows[0].reshape(length_all, kv_local, -1, head_size)
    attention = attend(
        grouped_q,
        joined[..., :head_size],
        joined[..., head_size:],
        block_count[my_index] * block_pool.shape[1],
        live_len,
    )
    ssm_out, attn_out = (
        lax.all_to_all(mamba[None], "tp", split_axis=1, concat_axis=2, tiled=True),
        lax.all_to_all(attention[None], "tp", split_axis=1, concat_axis=2, tiled=True),
    )
    return (ssm_out, attn_out)


def solution(mesh):
    return jax.shard_map(
        per_device,
        mesh=mesh,
        in_specs=(
            P("req", "tp", None),
            P("req", "tp", None),
            P("req", "tp", None),
            P("req", "tp", None),
            P("req", "tp", None),
            P("req", "tp", None),
            P("req", None, "tp", None),
            P("req", "tp", None, None),
            P("tp"),
            P("tp"),
            P("tp"),
            P("tp"),
            P(),
            P(),
            P(),
            P(),
            P(),
        ),
        out_specs=(P("req", "tp", None), P("req", "tp", None)),
        check_vma=False,
    )
```

profile of v0, /device:TPU:0, one launch (start us, length us, event | category | flops | bytes accessed | tf_op | source)
XLA Modules:
  0.0 608.4 jit_solution(11562995273234583211)
XLA Ops:
  18.5 11.5 %reduce.9 = bf16[2048,128]{1,0:T(8,128)(2,1)S(1)} reduce(bf16[2048,1,128]{2,1,0:T(2,128)(2,1)S(1)} %bitcast.301, bf16[]{:T(256)} %broadcast.338), dimensions={1}, to_apply=%bitcast.205.reduce_sub_computation | reduce | bytes 1048578
  37.9 22.4 %reduce.5 = bf16[4096,128]{1,0:T(8,128)(2,1)S(1)} reduce(bf16[4096,1,128]{2,1,0:T(2,128)(2,1)S(1)} %bitcast.294, bf16[]{:T(256)} %broadcast.338), dimensions={1}, to_apply=%bitcast.197.reduce_sub_computation | reduce | bytes 2097154
  70.9 23.4 %reduce.8 = bf16[4096,128]{1,0:T(8,128)(2,1)} reduce(bf16[4096,1,128]{2,1,0:T(2,128)(2,1)S(1)} %bitcast.295, bf16[]{:T(256)} %broadcast.338), dimensions={1}, to_apply=%bitcast.203.reduce_sub_computation | reduce | bytes 2097154
  102.1 6.9 %copy.256 = bf16[1,128,8192]{1,0,2:T(2,128)(2,1)} copy(bf16[1,128,8192]{2,1,0:T(8,128)(2,1)S(1)} %copy-done.7) | data formatting | bytes 4194304 | tf_op args[1]
  109.0 45.2 %reduce.6 = bf16[8192,128]{1,0:T(8,128)(2,1)S(1)} reduce(bf16[8192,1,128]{2,1,0:T(2,128)(2,1)} %bitcast.283, bf16[]{:T(256)} %broadcast.338), dimensions={1}, to_apply=%bitcast.199.reduce_sub_computation | reduce | bytes 4194306
  159.9 11.8 %all-gather.3.cloned.1.call-start = ((), (), s32[]{:S(2)}) async-start(), calls=%async_computation.8 | async-start | bytes 9437184 | tf_op jit(solution)/shard_map/all_gather | solution.py:140
  171.7 9.5 %copy.247 = bf16[1,128,8192]{1,0,2:T(2,128)(2,1)} copy(bf16[1,128,8192]{2,1,0:T(8,128)(2,1)} %param.21) | data formatting | bytes 4194304 | tf_op args[0]
  181.2 46.6 %reduce.4 = bf16[8192,128]{1,0:T(8,128)(2,1)} reduce(bf16[8192,1,128]{2,1,0:T(2,128)(2,1)} %bitcast.284, bf16[]{:T(256)} %broadcast.338), dimensions={1}, to_apply=%bitcast.195.reduce_sub_computation | reduce | bytes 4194306
  277.2 10.0 %copy.261 = f32[1,4,128,2048]{2,1,3,0:T(4,128)} copy(f32[1,4,128,2048]{2,3,1,0:T(8,128)S(1)} %convert_bitcast_fusion) | data formatting | bytes 8388608 | tf_op jit(solution)/shard_map/convert_element_type | solution.py:63
  287.2 5.5 copy.258
  300.2 11.1 %copy.248 = bf16[1,4,128,2048]{2,1,3,0:T(4,128)(2,1)} copy(bf16[1,4,128,2048]{2,3,1,0:T(8,128)(2,1)S(1)} %bitcast.287) | data formatting | bytes 4194304 | tf_op jit(solution)/shard_map/all_to_all | solution.py:132
  311.3 5.6 reshape_squeeze.12
  320.2 6.7 %reshape.362 = f32[2,256,2,16,64]{1,0,4,3,2:T(2,128)} reshape(f32[1,4,128,2048]{2,1,3,0:T(4,128)} %copy.261) | data formatting | bytes 8388608 | tf_op jit(solution)/shard_map/convert_element_type | solution.py:63
  326.9 5.4 copy.260
  342.4 114.7 %while.30 = (s32[]{:T(128)}, bf16[2,256,2,4,128]{4,3,2,1,0:T(4,128)(2,1)}, s32[2]{0:T(128)S(1)}, s32[]{:T(128)}, s32[]{:T(128)}, /*index=5*/bf16[512,2,4,128]{3,...) while((s32[]{:T(128)}, ...), condition=%wide.region_8.9_spmd.clone.clone, body=%wide.region_5.8_spmd.clone.clone.sunk | while | flops 4938803200 | bytes 125928624 | solution.py:107
  347.0 17.0 %bitcast_reduce_fusion.2 = (f32[2,4,256]{2,1,0:T(4,128)S(1)}, f32[2,256,4,4608]{3,1,2,0:T(8,128)}) fusion(pred[256,4608]{1,0:T(8,128)(4,1)S(1)} %compare_select_fusion.4, bf16[4608,2,128]{2,0,1:T(8,128)(2,1)} %get-tuple-element.656, bf16[256,2,4,128]{3,2,1,0:T(4,128)(2,1)S(1)} %constant_dynamic-slice_fusion.5), kind=kOutput, calls=%fused_computation.4.clone.1 | convolution fusion | flops 2444228608 | bytes 41820160 | tf_op jit(solution)/shard_map/while/body/eval_jaxpr/qcrd,kcd->crqk/dot_general | solution.py:86
  364.1 16.8 %fusion.113 = f32[2,4,256]{2,1,0:T(4,128)S(1)} fusion(f32[2,256,4,4608]{3,1,2,0:T(8,128)} %get-tuple-element.593, f32[2,4,256]{2,1,0:T(4,128)S(1)} %get-tuple-element.594, pred[256,4608]{1,0:T(8,128)(4,1)S(1)} %compare_select_fusion.4), kind=kLoop, calls=%fused_computation.7.clone.1 | loop fusion | flops 37746688 | bytes 38944768 | tf_op jit(solution)/shard_map/while/body/eval_jaxpr/reduce_sum | solution.py:98
  382.2 16.4 %fusion.114 = bf16[1,256,2,4,128]{4,1,3,2,0:T(8,128)(2,1)S(1)} fusion(bf16[4608,2,128]{2,0,1:T(8,128)(2,1)} %get-tuple-element.657, f32[2,256,4,4608]{3,1,2,0:T(8,128)} %get-tuple-element.593, f32[2,4,256]{2,1,0:T(4,128)S(1)} %get-tuple-element.594, pred[256,4608]{1,0:T(8,128)(4,1)S(1)} %compare_select_fusion.4, f32[256,2,4]{0,2,1:T(4,128)S(1)} %bitcast.306, ...), kind=kOutput, calls=%fused_computation.19.clone.1 | convolution fusion | flops 2454454272 | bytes 41828608 | tf_op jit(solution)/shard_map/while/body/eval_jaxpr/crqk,kcd->qcrd/dot_general | solution.py:100
  404.3 17.0 %bitcast_reduce_fusion.2 = (f32[2,4,256]{2,1,0:T(4,128)S(1)}, f32[2,256,4,4608]{3,1,2,0:T(8,128)}) fusion(pred[256,4608]{1,0:T(8,128)(4,1)S(1)} %compare_select_fusion.4, bf16[4608,2,128]{2,0,1:T(8,128)(2,1)} %get-tuple-element.656, bf16[256,2,4,128]{3,2,1,0:T(4,128)(2,1)S(1)} %constant_dynamic-slice_fusion.5), kind=kOutput, calls=%fused_computation.4.clone.1 | convolution fusion | flops 2444228608 | bytes 41820160 | tf_op jit(solution)/shard_map/while/body/eval_jaxpr/qcrd,kcd->crqk/dot_general | solution.py:86
  421.3 16.8 %fusion.113 = f32[2,4,256]{2,1,0:T(4,128)S(1)} fusion(f32[2,256,4,4608]{3,1,2,0:T(8,128)} %get-tuple-element.593, f32[2,4,256]{2,1,0:T(4,128)S(1)} %get-tuple-element.594, pred[256,4608]{1,0:T(8,128)(4,1)S(1)} %compare_select_fusion.4), kind=kLoop, calls=%fused_computation.7.clone.1 | loop fusion | flops 37746688 | bytes 38944768 | tf_op jit(solution)/shard_map/while/body/eval_jaxpr/reduce_sum | solution.py:98
  439.5 16.4 %fusion.114 = bf16[1,256,2,4,128]{4,1,3,2,0:T(8,128)(2,1)S(1)} fusion(bf16[4608,2,128]{2,0,1:T(8,128)(2,1)} %get-tuple-element.657, f32[2,256,4,4608]{3,1,2,0:T(8,128)} %get-tuple-element.593, f32[2,4,256]{2,1,0:T(4,128)S(1)} %get-tuple-element.594, pred[256,4608]{1,0:T(8,128)(4,1)S(1)} %compare_select_fusion.4, f32[256,2,4]{0,2,1:T(4,128)S(1)} %bitcast.306, ...), kind=kOutput, calls=%fused_computation.19.clone.1 | convolution fusion | flops 2454454272 | bytes 41828608 | tf_op jit(solution)/shard_map/while/body/eval_jaxpr/crqk,kcd->qcrd/dot_general | solution.py:100
  457.1 6.1 broadcast_in_dim_reshape.5
  463.2 6.8 %reduce.10 = bf16[512,1024]{1,0:T(8,128)(2,1)S(1)} reduce(bf16[512,1,1024]{2,1,0:T(2,128)(2,1)S(1)} %bitcast.292, bf16[]{:T(256)} %broadcast.338), dimensions={1}, to_apply=%bitcast.207.reduce_sub_computation | reduce | bytes 2097154
  476.5 9.4 %fusion.75 = f32[1,32,64,256]{3,0,2,1:T(1,128)S(1)} fusion(bf16[8,32,64,256]{3,2,1,0:T(8,128)(2,1)} %all-gather.3.cloned.1.call-done, s32[]{:T(128)} %bitcast.1), kind=kOutput, calls=%fused_computation.78 | convolution fusion | flops 8388616 | bytes 10485764 | tf_op jit(solution)/shard_map/e,emdn->mdn/dot_general | solution.py:142
  487.0 26.5 %while.29 = (s32[]{:T(128)}, f32[2,16,64,256]{3,2,1,0:T(8,128)S(1)}, f32[2,256,2,16,64]{1,4,3,2,0:T(8,128)}, f32[1,2,16]{2,1,0:T(2,128)S(1)}, f32[2,256,2,16]{1,...) while((s32[]{:T(128)}, ...), condition=%wide.region_3.4_spmd.clone, body=%wide.region_0.3_spmd.clone.sunk | while | flops 889815168 | bytes 30123316 | solution.py:61
  493.0 6.1 %fusion.110 = f32[2,256,2,16,64]{1,4,3,2,0:T(8,128)} fusion(f32[2,256,2,16,64]{1,4,3,2,0:T(8,128)} %get-tuple-element.608, s32[]{:T(128)} %get-tuple-element.606, f32[2,256,16,64]{1,3,2,0:T(8,128)} %fusion.109, f32[256,2,16]{0,2,1:T(8,128)S(1)} %bitcast.303, f32[256,256,2]{1,0,2:T(8,128)} %copy.338, f32[256,2,16]{0,2,1:T(8,128)S(1)} %bitcast_bitcast_fusion.2, ...), kind=kOutput, calls=%fused_computation.43.clone.1 | convolution fusion | flops 281542656 | bytes 7014400 | tf_op jit(solution)/shard_map/while/body/eval_jaxpr/tugh,ughp->tghp/dot_general | solution.py:46
  506.1 6.0 fusion.110
  513.5 7.5 %copy.255 = f32[2,256,2,16,64]{1,0,4,3,2:T(2,128)} copy(f32[2,256,2,16,64]{1,4,3,2,0:T(8,128)} %get-tuple-element.237) | data formatting | bytes 8388608 | tf_op jit(solution)/shard_map/while | solution.py:61
  521.0 6.4 %reshape.359 = f32[1,512,2048]{1,2,0:T(8,128)} reshape(f32[2,256,2,16,64]{1,0,4,3,2:T(2,128)} %copy.255) | data formatting | bytes 8388608 | tf_op jit(solution)/shard_map/reshape | solution.py:62
  534.9 7.7 %copy.264 = bf16[1,512,2048]{2,0,1:T(2,128)(2,1)} copy(bf16[1,512,2048]{1,2,0:T(8,128)(2,1)S(1)} %fusion.79) | data formatting | bytes 4194304 | tf_op jit(solution)/shard_map/convert_element_type | solution.py:72
  542.6 13.1 %reduce.7 = bf16[512,2048]{1,0:T(8,128)(2,1)S(1)} reduce(bf16[512,1,2048]{2,1,0:T(2,128)(2,1)} %bitcast.279, bf16[]{:T(256)} %broadcast.338), dimensions={1}, to_apply=%bitcast.201.reduce_sub_computation | reduce | bytes 4194306
  571.8 16.2 %all-to-all-done.4 = bf16[4,2,131072]{2,1,0:T(2,128)(2,1)S(1)} async-done(((bf16[4,2,131072]{2,1,0:T(2,128)(2,1)}), bf16[4,2,131072]{2,1,0:T(2,128)(2,1)S(1)}, u32[]{:S(2)}, u32[]{:S(2)}) %all-to-all-start.4) | async-done | bytes 2097184 | tf_op jit(solution)/shard_map/all_to_all | solution.py:183
  (191 shorter events, 181.0 us)
Async XLA Ops:
  7.2 27.9 %copy-start.9 = (bf16[1,128,4096]{2,1,0:T(8,128)(2,1)S(1)}, bf16[1,128,4096]{2,1,0:T(8,128)(2,1)}, u32[]{:S(2)}) copy-start(bf16[1,128,4096]{2,1,0:T(8,128)(2,1)} %param.23) | copy-start | bytes 3145732
  7.2 325.1 %all-gather.5.cloned.1.call-start = ((), (), s32[]{:S(2)}) async-start(), calls=%async_computation.9 | async-start | bytes 2359296 | tf_op jit(solution)/shard_map/all_gather | solution.py:164
  11.9 19.0 %all-to-all-start = ((bf16[4,2,2048]{2,1,0:T(2,128)(2,1)}), bf16[4,2,2048]{2,1,0:T(2,128)(2,1)S(1)}, u32[]{:S(2)}, u32[]{:S(2)}) async-start(bf16[4,2,2048]{2,1,0:T(2,128)(2,1)} %reshape.383), calls=%async_computation | async-start | bytes 65536 | tf_op jit(solution)/shard_map/all_to_all | solution.py:135
  30.9 31.0 %all-to-all-start.6 = ((bf16[4,2,32768]{2,1,0:T(2,128)(2,1)}), bf16[4,2,32768]{2,1,0:T(2,128)(2,1)}, u32[]{:S(2)}, u32[]{:S(2)}) async-start(bf16[4,2,32768]{2,1,0:T(2,128)(2,1)} %reshape.395), calls=%async_computation.6 | async-start | bytes 1048576 | tf_op jit(solution)/shard_map/all_to_all | solution.py:137
  61.9 35.9 %all-to-all-start.2 = ((bf16[4,2,65536]{2,1,0:T(2,128)(2,1)}), bf16[4,2,65536]{2,1,0:T(2,128)(2,1)S(1)}, u32[]{:S(2)}, u32[]{:S(2)}) async-start(bf16[4,2,65536]{2,1,0:T(2,128)(2,1)} %reshape.387), calls=%async_computation.2 | async-start | bytes 2097152 | tf_op jit(solution)/shard_map/all_to_all | solution.py:134
  94.2 7.9 %copy-start.7 = (bf16[1,128,8192]{2,1,0:T(8,128)(2,1)S(1)}, bf16[1,128,8192]{2,1,0:T(8,128)(2,1)}, u32[]{:S(2)}) copy-start(bf16[1,128,8192]{2,1,0:T(8,128)(2,1)} %param.22) | copy-start | bytes 6291460
  97.9 58.4 %all-to-all-start.5 = ((bf16[4,2,65536]{2,1,0:T(2,128)(2,1)}), bf16[4,2,65536]{2,1,0:T(2,128)(2,1)}, u32[]{:S(2)}, u32[]{:S(2)}) async-start(bf16[4,2,65536]{2,1,0:T(2,128)(2,1)} %reshape.393), calls=%async_computation.5 | async-start | bytes 2097152 | tf_op jit(solution)/shard_map/all_to_all | solution.py:136
  156.3 81.1 %all-to-all-start.3 = ((bf16[4,2,131072]{2,1,0:T(2,128)(2,1)}), bf16[4,2,131072]{2,1,0:T(2,128)(2,1)S(1)}, u32[]{:S(2)}, u32[]{:S(2)}) async-start(bf16[4,2,131072]{2,1,0:T(2,128)(2,1)} %reshape.389), calls=%async_computation.3 | async-start | bytes 4194304 | tf_op jit(solution)/shard_map/all_to_all | solution.py:133
  159.9 316.6 %all-gather.3.cloned.1.call-start = ((), (), s32[]{:S(2)}) async-start(), calls=%async_computation.8 | async-start | bytes 9437184 | tf_op jit(solution)/shard_map/all_gather | solution.py:140
  181.2 50.7 %copy-start.14 = (f32[32]{0:T(128)S(1)}, f32[32]{0:T(128)}, u32[]{:S(2)}) copy-start(f32[32]{0:T(128)} %param.30) | copy-start | bytes 388
  181.2 50.7 %copy-start.15 = (f32[32]{0:T(128)S(1)}, f32[32]{0:T(128)}, u32[]{:S(2)}) copy-start(f32[32]{0:T(128)} %param.29) | copy-start | bytes 388
  181.2 51.4 %copy-start.16 = (s32[8]{0:T(128)S(1)}, s32[8]{0:T(128)}, u32[]{:S(2)}) copy-start(s32[8]{0:T(128)} %param.36) | copy-start | bytes 100
  181.2 52.0 %copy-start.17 = (s32[8]{0:T(128)S(1)}, s32[8]{0:T(128)}, u32[]{:S(2)}) copy-start(s32[8]{0:T(128)} %param.37) | copy-start | bytes 100
  181.2 53.5 %copy-start.18 = (s32[8]{0:T(128)S(1)}, s32[8]{0:T(128)}, u32[]{:S(2)}) copy-start(s32[8]{0:T(128)} %param.35) | copy-start | bytes 100
  237.4 13.1 %copy-start.6 = (bf16[4,2,131072]{2,1,0:T(2,128)(2,1)}, bf16[4,2,131072]{2,1,0:T(2,128)(2,1)S(1)}, u32[]{:S(2)}) copy-start(bf16[4,2,131072]{2,1,0:T(2,128)(2,1)S(1)} %all-to-all-done.3) | copy-start | bytes 6291460
  237.4 55.3 %all-to-all-start.1 = ((bf16[4,2,131072]{2,1,0:T(2,128)(2,1)}), bf16[4,2,131072]{2,1,0:T(2,128)(2,1)}, u32[]{:S(2)}, u32[]{:S(2)}) async-start(bf16[4,2,131072]{2,1,0:T(2,128)(2,1)} %reshape.385), calls=%async_computation.1 | async-start | bytes 4194304 | tf_op jit(solution)/shard_map/all_to_all | solution.py:132
  275.2 2.0 copy-start
  339.1 1.0 copy-start.8
  471.9 86.6 %all-to-all-start.7 = ((bf16[4,2,65536]{2,1,0:T(2,128)(2,1)}), bf16[4,2,65536]{2,1,0:T(2,128)(2,1)}, u32[]{:S(2)}, u32[]{:S(2)}) async-start(bf16[4,2,65536]{2,1,0:T(2,128)(2,1)} %reshape.397), calls=%async_computation.7 | async-start | bytes 2097152 | tf_op jit(solution)/shard_map/all_to_all | solution.py:184
  485.9 1.0 copy-start.2
  485.9 1.0 copy-start.10
  485.9 1.0 copy-start.11
  485.9 1.0 copy-start.19
  493.0 6.1 %copy-start.1 = (bf16[2,256,2,16,64]{1,4,3,2,0:T(8,128)(2,1)S(1)}, bf16[2,256,2,16,64]{1,4,3,2,0:T(8,128)(2,1)}, u32[]{:S(2)}) copy-start(bf16[2,256,2,16,64]{1,4,3,2,0:T(8,128)(2,1)} %get-tuple-element.622) | copy-start | bytes 6291460 | tf_op jit(solution)/shard_map/while
  493.0 6.1 %copy-start.3 = (bf16[2,256,2,256]{3,1,2,0:T(8,128)(2,1)S(1)}, bf16[2,256,2,256]{3,1,2,0:T(8,128)(2,1)}, u32[]{:S(2)}) copy-start(bf16[2,256,2,256]{3,1,2,0:T(8,128)(2,1)} %get-tuple-element.623) | copy-start | bytes 1572868 | tf_op jit(solution)/shard_map/while
  506.0 6.0 copy-start.1
  506.0 6.0 copy-start.3
  527.4 4.8 copy-start.4
  527.4 5.9 copy-start.5
  527.5 5.9 copy-start.12
  527.5 5.9 copy-start.13
  558.5 29.5 %all-to-all-start.4 = ((bf16[4,2,131072]{2,1,0:T(2,128)(2,1)}), bf16[4,2,131072]{2,1,0:T(2,128)(2,1)S(1)}, u32[]{:S(2)}, u32[]{:S(2)}) async-start(bf16[4,2,131072]{2,1,0:T(2,128)(2,1)} %reshape.391), calls=%async_computation.4 | async-start | bytes 4194304 | tf_op jit(solution)/shard_map/all_to_all | solution.py:183
Sparse Core Ops, SparseCore 0:
  10.1 51.9 all-gather.4
  171.8 127.1 all-gather.2
where the time goes:
time: 620 us; the launch traced here: 608 us
  other arithmetic  225 us (36%)
  local copies, waits for them, and re-layouts  206 us (33%)
  matrix products  96.3 us (16%)
  starting transfers between devices  44.7 us (7%)
  waiting for transfers between devices  16.2 us (3%)
  between operations  15.3 us (2%)
    unnamed x8, other arithmetic  170 us
    unnamed x69, local copies, waits for them, and re-layouts  96.8 us
    dot_general x2, matrix products, one_block(): jnp.einsum('qcrd,kcd->crqk', block_q, key_rows, preferred_element_type=jn...  34.1 us
    reduce_sum x2, other arithmetic, one_block(): totals = jnp.sum(expon, axis=-1)  33.6 us
    dot_general x2, matrix products, one_block(): jnp.einsum('crqk,kcd->qcrd', weights, value_rows, preferred_element_type=...  32.8 us
    convert_element_type x4, local copies, waits for them, and re-layouts, scan_heads(): gate_rows.astype(jnp.float32)  27.6 us
    all_to_all x1, waiting for transfers between devices, per_device(): lax.all_to_all(mamba[None], 'tp', split_axis=1, concat_axis=2, tiled=True)  16.2 us
  transfers between devices with their start and end apart: 10, of which 1 were waited for; matrix products, arithmetic and copies ran while one was open for 84% of the time, Pallas kernels for 0%

commit v1 on v0

v1 whole, which is shorter than its diff:
```python
import functools
import math

import jax
import jax.numpy as jnp
from jax import lax
from jax.experimental import pallas as pl
from jax.experimental.pallas import tpu as pltpu
from jax.sharding import PartitionSpec as P

STATE = 256
SPAN = 256
TILE = 256
VMEM = 60 * 1024 * 1024
SMALL = 8 * 1024 * 1024


def cost(microseconds=0.0):
    return pl.CostEstimate(
        flops=1024 + int(microseconds * 1.15e9), bytes_accessed=1024, transcendentals=0
    )


def params(limit=VMEM):
    return pltpu.CompilerParams(vmem_limit_bytes=limit)


def dot_nt(left, right):
    return lax.dot_general(left, right, (((1,), (1,)), ((), ())), preferred_element_type=jnp.float32)


def dot_tn(left, right):
    return lax.dot_general(left, right, (((0,), (0,)), ((), ())), preferred_element_type=jnp.float32)


def pack(parts, pieces, gain):
    rows = pieces[0][0].shape[0]
    widths = [width for _, width, _ in pieces]
    gain_rows, lanes = gain.shape
    total = sum(widths) + lanes

    def body(*refs):
        *piece_refs, gain_ref, out_ref = refs
        at = 0
        for ref, width in zip(piece_refs, widths):
            out_ref[:, at : at + width] = ref[...]
            at += width
        terms, rest = [], gain_ref[...]
        for _ in range(3):
            terms.append(rest.astype(jnp.bfloat16).astype(jnp.float32))
            rest = rest - terms[-1]
        terms.append(jnp.zeros((rows - 3 * gain_rows, lanes), jnp.float32))
        out_ref[:, at:] = jnp.concatenate(terms, axis=0).astype(jnp.bfloat16)

    specs = [
        pl.BlockSpec((rows, width), functools.partial(lambda place, p: (0, place(p)), place))
        for _, width, place in pieces
    ]
    return pl.pallas_call(
        body,
        grid=(parts,),
        in_specs=specs + [pl.BlockSpec(gain.shape, lambda p: (0, 0))],
        out_specs=pl.BlockSpec((None, rows, total), lambda p: (p, 0, 0)),
        out_shape=jax.ShapeDtypeStruct((parts, rows, total), jnp.bfloat16),
        compiler_params=params(),
        cost_estimate=cost(),
    )(*[array for array, _, _ in pieces], gain)


def spread(packed):
    return lax.all_to_all(packed, "tp", split_axis=0, concat_axis=0, tiled=True)


def swap(value, axis, mask):
    count = lax.axis_size(axis)
    return lax.ppermute(value, axis, [(i, i ^ mask) for i in range(count)])


def exchange(buffers):
    return [buffers[0]] + [swap(buffers[k], "tp", k) for k in range(1, len(buffers))]


def after(value, *others):
    return lax.optimization_barrier((value, *others))[0]


def join_body(one_ref, two_ref, out_ref):
    half = one_ref.shape[0]
    out_ref[:half] = one_ref[...]
    out_ref[half:] = two_ref[...]


def join(one, two):
    shape = (one.shape[0] + two.shape[0],) + one.shape[1:]
    return pl.pallas_call(
        join_body,
        out_shape=jax.ShapeDtypeStruct(shape, one.dtype),
        compiler_params=params(SMALL),
        cost_estimate=cost(15),
    )(one, two)


def block_places(targets, used_entries, pool_total):
    blocks = jnp.arange(pool_total, dtype=jnp.int32)
    live = jnp.arange(targets.shape[0]) < used_entries
    named = (targets[:, None] == blocks[None, :]) & live[:, None]
    often = jnp.sum(named.astype(jnp.int32), axis=0)
    used = often > 0
    place = jnp.sum((used[None, :] & (blocks[None, :] < blocks[:, None])).astype(jnp.int32), axis=1)
    total = jnp.sum(used.astype(jnp.int32))
    return often, place.astype(jnp.int32), total.astype(jnp.int32)


def attention_body(parts, pool_offsets, listed, size, where_ref, often_ref, place_ref, q_ref, fresh_ref, *refs):
    pool_refs = refs[: len(pool_offsets)]
    out_ref, key_ref, value_ref = refs[len(pool_offsets) :]
    rows = q_ref.shape[1]
    repeat = q_ref.shape[2] // size
    fresh, block = fresh_ref.shape[0], pool_refs[0].shape[1]
    prefix = listed * block
    scale = math.log2(math.e) / math.sqrt(size)
    request, total = where_ref[0], where_ref[1]

    for pool_ref, offsets in zip(pool_refs, pool_offsets):
        slots = pool_ref.shape[0] // len(offsets)
        for index, offset in enumerate(offsets):
            for slot in range(slots):
                number = (request ^ offset) * slots + slot
                times = often_ref[number]

                @pl.when(times > 0)
                def _(pool_ref=pool_ref, held=index * slots + slot, number=number, times=times):
                    at = pl.ds(pl.multiple_of(place_ref[number] * block, block), block)
                    pair = pool_ref[held]
                    often = times.astype(jnp.float32)
                    key_ref[at, :] = pair[:, :size]
                    value_ref[at, :size] = (pair[:, size:].astype(jnp.float32) * often).astype(jnp.bfloat16)
                    value_ref[at, size:] = jnp.full((block, size), often, jnp.float32).astype(jnp.bfloat16)

    def fill(step, carry):
        at = pl.ds(pl.multiple_of(step * block, block), block)
        key_ref[at, :] = key_ref[:block, :]
        value_ref[at, :] = jnp.zeros((block, 2 * size), jnp.bfloat16)
        return carry

    lax.fori_loop(total, listed, fill, 0)
    key_ref[prefix:, :] = fresh_ref[:, :size]
    value_ref[prefix:, :size] = fresh_ref[:, size:]
    value_ref[prefix:, size:] = jnp.ones((fresh, size), jnp.bfloat16)

    query_at = lax.broadcasted_iota(jnp.int32, (repeat, rows, rows), 1).reshape(repeat * rows, rows)
    below = lax.broadcasted_iota(jnp.int32, (repeat * rows, rows), 1) <= query_at

    def scores(k):
        queries = jnp.concatenate(
            [q_ref[k, :, head * size : (head + 1) * size] for head in range(repeat)], axis=0
        )
        whole = prefix + k * rows
        return dot_nt(queries, key_ref[:whole, :]), dot_nt(queries, key_ref[whole : whole + rows, :])

    following = scores(0)
    for k in range(parts):
        seen, edge = following
        if k + 1 < parts:
            following = scores(k + 1)
        whole = prefix + k * rows
        edge = jnp.where(below, edge, -jnp.inf)
        top = jnp.maximum(
            jnp.max(seen, axis=1, keepdims=True), jnp.max(edge, axis=1, keepdims=True)
        )
        seen = jnp.exp2((seen - top) * scale).astype(jnp.bfloat16)
        edge = jnp.exp2((edge - top) * scale).astype(jnp.bfloat16)
        mixed = jnp.dot(seen, value_ref[:whole, :], preferred_element_type=jnp.float32)
        mixed += jnp.dot(edge, value_ref[whole : whole + rows, :], preferred_element_type=jnp.float32)
        result = (mixed[:, :size] / mixed[:, size:]).astype(jnp.bfloat16)
        for head in range(repeat):
            out_ref[k, :, head * size : (head + 1) * size] = result[head * rows : (head + 1) * rows]


def attention(first, pools, where, often, place, listed, q_column, q_width):
    parts, rows, _ = first.shape
    _, kv_local, block, pair = pools[0][0].shape
    size = pair // 2
    per_kv = q_width // kv_local
    keys = listed * block + rows * parts
    specs = [
        pl.BlockSpec((parts, rows, per_kv), lambda c, *_: (0, 0, q_column // per_kv + c)),
        pl.BlockSpec((rows * parts, pair), lambda c, *_: (0, (q_column + q_width) // pair + c)),
    ]
    specs += [
        pl.BlockSpec((array.shape[0], None, block, pair), lambda c, *_: (0, c, 0, 0)) for array, _ in pools
    ]
    return pl.pallas_call(
        functools.partial(attention_body, parts, [offsets for _, offsets in pools], listed, size),
        grid_spec=pltpu.PrefetchScalarGridSpec(
            num_scalar_prefetch=3,
            grid=(kv_local,),
            in_specs=specs,
            out_specs=pl.BlockSpec((parts, rows, per_kv), lambda c, *_: (0, 0, c)),
            scratch_shapes=[
                pltpu.VMEM((keys, size), jnp.bfloat16),
                pltpu.VMEM((keys, 2 * size), jnp.bfloat16),
            ],
        ),
        out_shape=jax.ShapeDtypeStruct((parts, rows, q_width), jnp.bfloat16),
        compiler_params=params(),
        cost_estimate=cost(16),
    )(
        where,
        often,
        place,
        first,
        first.reshape(parts * rows, first.shape[2]),
        *[array for array, _ in pools],
    )


def scan_body(parts, sources, heads, group, where_ref, x_ref, proj_ref, raw_ref, head_ref, skip_ref, *refs):
    state_refs = refs[:sources]
    out_refs = refs[sources:-4]
    y_ref, state_ref, next_ref, sem = refs[-4:]
    share = where_ref[0]
    shift = where_ref[1]
    source = where_ref[2]
    rows, width = x_ref.shape
    for index in range(sources):

        @pl.when(source == index)
        def _(index=index):
            pltpu.make_async_copy(rows_of(state_refs[index], group, width), state_ref, sem).start()

    channels = width // heads
    lane = lax.broadcasted_iota(jnp.int32, (1, 2 * channels), 1)
    first_lanes = lane < channels
    row_at = lax.broadcasted_iota(jnp.int32, (2 * channels, 1), 0)
    first_rows = row_at < channels
    lower = lax.broadcasted_iota(jnp.int32, (SPAN, SPAN), 1) <= lax.broadcasted_iota(
        jnp.int32, (SPAN, SPAN), 0
    )
    base = math.log2(math.e)
    ones = jnp.where(lower, 1.0, 0.0)
    raw = pltpu.roll(raw_ref[...].astype(jnp.float32), shift, 1) + head_ref[1:2, :]
    step = jnp.maximum(raw, 0.0) + jnp.log1p(jnp.exp(-jnp.abs(raw)))
    rates = jnp.exp(head_ref[0:1, :])
    for start in range(0, rows, SPAN):
        at = slice(start, start + SPAN)
        last_block = start + SPAN >= rows
        step_block = step[at, :]
        cumul = jnp.dot(
            ones,
            -rates * step_block,
            precision=lax.Precision.HIGHEST,
            preferred_element_type=jnp.float32,
        )
        ahead = base * cumul
        back = jnp.transpose(base * (jnp.log(step_block) - cumul))
        grown = jnp.exp(cumul)
        final = cumul[SPAN - 1 : SPAN, :]
        tail = jnp.exp(final - cumul) * step_block
        kept = jnp.exp(final)
        b_block = proj_ref[at, :STATE]
        c_block = proj_ref[at, STATE:]
        inner = dot_nt(c_block, b_block)
        if start == 0:
            pltpu.make_async_copy(rows_of(state_refs[0], group, width), state_ref, sem).wait()
        state = state_ref if start == 0 else next_ref
        carried = dot_nt(c_block, state[...])
        for pair in range(heads // 2):
            cols = slice(pair * 2 * channels, (pair + 1) * 2 * channels)
            one, two = 2 * pair, 2 * pair + 1
            x_pair = x_ref[at, cols]
            mixings = []
            for head in (one, two):
                spread_at = ahead[:, head : head + 1] + back[head : head + 1, :]
                decay = jnp.exp2(jnp.where(lower, spread_at, -jnp.inf))
                mixings.append((decay * inner).astype(jnp.bfloat16))
            nothing = jnp.zeros_like(x_pair)
            output = jnp.dot(
                mixings[0], jnp.where(first_lanes, x_pair, nothing), preferred_element_type=jnp.float32
            )
            output += jnp.dot(
                mixings[1], jnp.where(first_lanes, nothing, x_pair), preferred_element_type=jnp.float32
            )
            x_wide = x_pair.astype(jnp.float32)
            factor = jnp.where(first_lanes, grown[:, one : one + 1], grown[:, two : two + 1])
            output += factor * carried[:, cols] + skip_ref[:, cols] * x_wide
            y_ref[at, cols] = output.astype(jnp.bfloat16)
            if not last_block:
                weight = jnp.where(first_lanes, tail[:, one : one + 1], tail[:, two : two + 1])
                terms = (weight * x_wide).astype(jnp.bfloat16)
                keep = jnp.where(first_rows, kept[:, one : one + 1], kept[:, two : two + 1])
                moved = keep * state[cols, :].astype(jnp.float32) + dot_tn(terms, b_block)
                next_ref[cols, :] = moved.astype(jnp.bfloat16)
    part_rows = rows // parts
    for k in range(parts):
        at = pl.ds(pl.multiple_of((share ^ k) * part_rows, part_rows), part_rows)
        out_refs[k][...] = y_ref[at, :]


def scan_group(joined, step_column, states, where, head_rows, skip_row, heads, group, local_groups):
    parts, part_rows, _ = joined.shape
    sources = len(states)
    rows = part_rows * parts
    width = skip_row.shape[1]
    step_width = head_rows.shape[1]
    proj_width = 2 * STATE
    specs = [
        pl.BlockSpec((rows, width), lambda i, *_: (0, group)),
        pl.BlockSpec((rows, proj_width), lambda i, *_: (0, local_groups * width // proj_width + group)),
        pl.BlockSpec((rows, step_width), lambda i, *_: (0, step_column // step_width)),
        pl.BlockSpec((8, step_width), lambda i, *_: (0, 0)),
        pl.BlockSpec((1, width), lambda i, *_: (0, 0)),
    ]
    specs += [pl.BlockSpec(memory_space=pl.ANY)] * sources
    flat = joined.reshape(rows, joined.shape[2])
    return pl.pallas_call(
        functools.partial(scan_body, parts, sources, heads, group),
        grid_spec=pltpu.PrefetchScalarGridSpec(
            num_scalar_prefetch=1,
            grid=(1,),
            in_specs=specs,
            out_specs=[pl.BlockSpec((part_rows, width), lambda i, *_: (0, 0))] * parts,
            scratch_shapes=[
                pltpu.VMEM((rows, width), jnp.bfloat16),
                pltpu.VMEM((width, STATE), jnp.bfloat16),
                pltpu.VMEM((width, STATE), jnp.bfloat16),
                pltpu.SemaphoreType.DMA,
            ],
        ),
        out_shape=[jax.ShapeDtypeStruct((part_rows, width), jnp.bfloat16)] * parts,
        compiler_params=params(),
        cost_estimate=cost(8),
    )(where, flat, flat, flat, head_rows, skip_row, *states)


def rows_of(ref, group, size):
    return ref if ref.shape[0] == size else ref.at[group * size : (group + 1) * size]


def choose_body(sources, group, index_ref, *refs):
    out_ref, sem = refs[sources:]
    size = out_ref.shape[0]
    for index in range(sources):

        @pl.when(index_ref[0] == index)
        def _(index=index):
            pltpu.make_async_copy(rows_of(refs[index], group, size), out_ref, sem).start()

    pltpu.make_async_copy(rows_of(refs[0], group, size), out_ref, sem).wait()


def choose(index, arrays, group, size):
    return pl.pallas_call(
        functools.partial(choose_body, len(arrays), group),
        grid_spec=pltpu.PrefetchScalarGridSpec(
            num_scalar_prefetch=1,
            grid=(1,),
            in_specs=[pl.BlockSpec(memory_space=pl.ANY)] * len(arrays),
            out_specs=pl.BlockSpec((size, STATE), lambda i, *_: (0, 0)),
            scratch_shapes=[pltpu.SemaphoreType.DMA],
        ),
        out_shape=jax.ShapeDtypeStruct((size, STATE), jnp.bfloat16),
        compiler_params=params(SMALL),
        cost_estimate=cost(),
    )(index, *arrays)


def bit_order(count, group):
    bits = count.bit_length() - 1
    if group % 2 == 0:
        return [bits - 1] + list(range(bits - 1))
    return [bits - 2] + list(range(bits - 2)) + [bits - 1]


def slot_of(distance, offsets):
    return sum(jnp.where(distance == offset, i, 0) for i, offset in enumerate(offsets))


def fetch_state(own, far, far_mask, entries, order, gate, late_gate, group):
    count = lax.axis_size("req")
    size = own.shape[0]
    offsets, held = [0], [own]
    for step, bit in enumerate(order[:-1]):
        mask = 1 << bit
        moved = []
        for offset, value in zip(offsets, held):
            if offset == 0 and mask == far_mask:
                moved.append(far)
            else:
                moved.append(swap(after(value, *(late_gate if step else gate)), "req", mask))
        held = held + moved
        offsets = offsets + [offset ^ mask for offset in offsets]
    last = 1 << order[-1]
    every = jnp.arange(count, dtype=jnp.int32)
    bits = len(order)
    flipped = jnp.flip(entries.reshape((2,) * bits), bits - 1 - order[-1]).reshape(count)
    distance = entries ^ every
    source = jnp.where((distance & last) == 0, slot_of(distance, offsets), len(held))
    choices = jnp.stack([slot_of(flipped ^ every, offsets), source]).astype(jnp.int32)
    mine = lax.dynamic_slice_in_dim(choices, lax.axis_index("req"), 1, axis=1)[:, 0]
    begun = choose(mine[0:1], held, group, size)
    return mine[1], held + [swap(begun, "req", last)], begun


def norm_body(parts, group, local_groups, where_ref, *refs):
    y_refs = refs[:parts]
    gate_refs = refs[parts : 2 * parts]
    gain_refs = refs[2 * parts : 3 * parts]
    out_ref, done_ref, sem = refs[-3:]
    share, live = where_ref[0], where_ref[1]
    number, steps = pl.program_id(0), pl.num_programs(0)
    rows, width = y_refs[0].shape
    row_at = lax.broadcasted_iota(jnp.int32, (rows, 1), 0) + number * rows
    lanes = gain_refs[0].shape[1]
    chunks = width // lanes
    third = chunks * local_groups

    def placing(step, k):
        column = pl.multiple_of(((share ^ k) * local_groups + group) * width, width)
        at = pl.ds(pl.multiple_of(step * rows, rows), rows)
        return pltpu.make_async_copy(done_ref.at[step, k], out_ref.at[at, pl.ds(column, width)], sem.at[step, k])

    for k in range(parts):
        gate = gate_refs[k][...].astype(jnp.float32)
        gated = y_refs[k][...].astype(jnp.float32) * gate * (0.5 + 0.5 * jnp.tanh(0.5 * gate))
        mean_sq = jnp.mean(gated * gated, axis=1, keepdims=True)
        normed = gated * jnp.where(row_at < live, lax.rsqrt(mean_sq + 1e-05), 0.0)
        gains = gain_refs[k][...].astype(jnp.float32)
        first = group * chunks
        gain = sum(gains[first + i * third : first + i * third + chunks] for i in range(3))
        for chunk in range(chunks):
            cols = slice(chunk * lanes, (chunk + 1) * lanes)
            done_ref[number, k, :, cols] = (normed[:, cols] * gain[chunk : chunk + 1, :]).astype(jnp.bfloat16)
        placing(number, k).start()

    @pl.when(number == steps - 1)
    def _():
        for step in range(done_ref.shape[0]):
            for k in range(parts):
                placing(step, k).wait()


def norm_group(returned, gate, joined, where, group, local_groups, earlier):
    parts = joined.shape[0]
    rows, width = returned[0].shape[-2:]
    lanes, steps = 128, 2
    step = rows // steps
    specs = [pl.BlockSpec((step, width), lambda i, *_: (i, 0))] * parts
    specs += [
        pl.BlockSpec((step, width), functools.partial(lambda k, i, at: (i, (at[0] ^ k) * local_groups + group), k))
        for k in range(parts)
    ]
    specs += [
        pl.BlockSpec(
            (None, rows, lanes),
            functools.partial(lambda k, i, at: (at[0] ^ k, 0, joined.shape[2] // lanes - 1), k),
        )
        for k in range(parts)
    ]
    inputs = [where, *returned, *([gate] * parts), *([joined] * parts)]
    aliases = {}
    if earlier is not None:
        aliases = {len(inputs): 0}
        inputs.append(earlier)
        specs.append(pl.BlockSpec(memory_space=pl.ANY))
    return pl.pallas_call(
        functools.partial(norm_body, parts, group, local_groups),
        grid_spec=pltpu.PrefetchScalarGridSpec(
            num_scalar_prefetch=1,
            grid=(steps,),
            in_specs=specs,
            out_specs=pl.BlockSpec(memory_space=pl.ANY),
            scratch_shapes=[
                pltpu.VMEM((steps, parts, step, width), jnp.bfloat16),
                pltpu.SemaphoreType.DMA((steps, parts)),
            ],
        ),
        out_shape=jax.ShapeDtypeStruct(gate.shape, jnp.bfloat16),
        input_output_aliases=aliases,
        compiler_params=params(),
        cost_estimate=cost(3),
    )(*inputs)


def place_body(where_ref, in_ref, out_ref):
    parts, rows, width = in_ref.shape
    alive = lax.broadcasted_iota(jnp.int32, (rows, 1), 0) + pl.program_id(0) * rows < where_ref[1]
    for part in range(parts):
        value = in_ref[part].astype(jnp.float32)
        out_ref[:, part * width : (part + 1) * width] = jnp.where(alive, value, 0.0).astype(jnp.bfloat16)


def place_heads(returned, where):
    parts, rows, width = returned.shape
    step = rows // 2
    return pl.pallas_call(
        place_body,
        grid_spec=pltpu.PrefetchScalarGridSpec(
            num_scalar_prefetch=1,
            grid=(rows // step,),
            in_specs=[pl.BlockSpec((parts, step, width), lambda i, *_: (0, i, 0))],
            out_specs=pl.BlockSpec((step, parts * width), lambda i, *_: (i, 0)),
        ),
        out_shape=jax.ShapeDtypeStruct((rows, parts * width), jnp.bfloat16),
        compiler_params=params(),
        cost_estimate=cost(2),
    )(where, returned)


def per_device(
    ssm_input,
    ssm_gate,
    state_proj,
    step_raw,
    queries,
    fresh_kv,
    block_pool,
    state_pool,
    decay_log,
    step_bias,
    skip_gain,
    norm_gain,
    block_owner,
    block_slot,
    block_count,
    state_entry,
    suffix_len,
):
    request = lax.axis_index("req")
    share = lax.axis_index("tp")
    parts = lax.axis_size("tp")
    owners = lax.axis_size("req")
    rows = ssm_input.shape[1]
    groups = state_proj.shape[2] // (2 * STATE)
    local_groups = groups // parts
    group_width = ssm_input.shape[2] // groups
    head_total = step_raw.shape[2]
    heads = head_total // groups
    channels = group_width // heads
    q_width = queries.shape[2] // parts
    fresh_width = fresh_kv.shape[2] // parts
    pool_local = block_pool.shape[0]
    pool_total = pool_local * owners
    listed = min(block_owner.shape[1], pool_total)
    order = bit_order(owners, 0)
    first_bit = 1 << order[0]

    pieces = [
        (ssm_input[0], local_groups * group_width, lambda p: p),
        (state_proj[0], local_groups * 2 * STATE, lambda p: p),
        (queries[0], q_width, lambda p: p),
        (fresh_kv[0], fresh_width, lambda p: p),
        (step_raw[0], head_total, lambda p: 0),
    ]
    q_column = pieces[0][1] + pieces[1][1]
    step_column = q_column + q_width + fresh_width
    pool_own = jnp.transpose(block_pool, (0, 2, 1, 3))
    state_own = state_pool.reshape(local_groups * group_width, STATE)
    state_groups = [state_own[group * group_width : (group + 1) * group_width] for group in range(local_groups)]
    packed = pack(parts, pieces, after(norm_gain, pool_own, *state_groups).reshape(-1, 128))
    joined = spread(packed)

    far_mask = 1 << order[1]
    state_far = swap(state_own, "req", far_mask)
    pool_far = after(swap(pool_own, "req", first_bit), packed)
    pool_held = join(pool_own, pool_far)
    pools = [(pool_held, [0, first_bit])]
    for bit in [order[-1]] + order[1:-1]:
        mask = 1 << bit
        moved = []
        for index, (array, held) in enumerate(pools):
            gate = [state_far] if mask == far_mask and index > 0 else []
            moved.append((swap(after(array, *gate), "req", mask), [offset ^ mask for offset in held]))
        pools += moved

    entries = after(state_entry, pool_held)
    state_lists, begun, late_gate = [None] * local_groups, [], [array for array, _ in pools[1:3]]
    for group in reversed(range(local_groups)):
        gates = ([pool_far], late_gate) if group % 2 == 0 else ([], [])
        source, values, sent = fetch_state(
            state_groups[group], state_far, far_mask, entries, bit_order(owners, group), *gates, group
        )
        state_lists[group] = (source, values)
        begun.append(sent)
        late_gate = late_gate + [values[-2]]

    targets = after(block_owner, pool_held)[request] * pool_local + block_slot[request]
    often, place, total = block_places(targets, block_count[request], pool_total)
    where = jnp.stack([request, total]).astype(jnp.int32)
    live = jnp.stack([share, suffix_len[request] - share * rows]).astype(jnp.int32)

    where = after(where, *begun[:-1])
    mixed = attention(joined, pools, where, often, place, listed, q_column, q_width)
    attn_back = spread(mixed)

    ssm_out = None
    skips = jnp.repeat(skip_gain, channels)[None, :]
    for group in reversed(range(local_groups)):
        mine = slice(group * heads, (group + 1) * heads)
        head_rows = jnp.zeros((8, head_total), jnp.float32)
        head_rows = head_rows.at[0, :heads].set(decay_log[mine])
        head_rows = head_rows.at[1, :heads].set(step_bias[mine])
        start = (share * local_groups + group) * heads
        shift = lax.rem(head_total - start, head_total)
        cols = slice(group * group_width, (group + 1) * group_width)
        source, values = state_lists[group]
        where = after(jnp.stack([share, shift, source]).astype(jnp.int32), mixed)
        scanned = scan_group(
            joined, step_column, values, where, head_rows, skips[:, cols], heads, group, local_groups
        )
        if group == 0:
            attn_out = place_heads(attn_back, after(live, scanned[0]))
            live = after(live, attn_out)
        ssm_out = norm_group(exchange(scanned), ssm_gate[0], joined, live, group, local_groups, ssm_out)
    return (ssm_out[None], attn_out[None])


def solution(mesh):
    return jax.shard_map(
        per_device,
        mesh=mesh,
        in_specs=(
            P("req", "tp", None),
            P("req", "tp", None),
            P("req", "tp", None),
            P("req", "tp", None),
            P("req", "tp", None),
            P("req", "tp", None),
            P("req", None, "tp", None),
            P("req", "tp", None, None),
            P("tp"),
            P("tp"),
            P("tp"),
            P("tp"),
            P(),
            P(),
            P(),
            P(),
            P(),
        ),
        out_specs=(P("req", "tp", None), P("req", "tp", None)),
        check_vma=False,
    )
```

time: 620 us -> 141 us (0.23); the launches traced: 608 us -> 140 us
  other arithmetic: 225 us -> 7.31 us
  local copies, waits for them, and re-layouts: 206 us -> 9.64 us
  matrix products: 96.3 us -> 0 us
  Pallas kernels: 0 us -> 52.8 us
  waiting for transfers between devices: 16.2 us -> 41.7 us
  starting transfers between devices: 44.7 us -> 27.2 us
  between operations: 15.3 us -> 1.81 us
    unnamed x8 -> x0, other arithmetic: 170 us -> none
    dot_general x13 -> x0, matrix products: 96.3 us -> none  [the longest x2 34.1 us: one_block(): jnp.einsum('qcrd,kcd->crqk', block_q, key_rows, preferred_element_type=jn...]
    unnamed x69 -> x49, local copies, waits for them, and re-layouts: 96.8 us -> 4.25 us
    pallas_call x0 -> x10, Pallas kernels: none -> 52.8 us  [the longest x2 17.7 us: scan_group(): pl.pallas_call(functools.partial(scan_body, parts, sources, heads, group)...]
    ppermute x0 -> x17, waiting for transfers between devices: none -> 41.7 us  [swap(): return lax.ppermute(value, axis, [(i, i ^ mask) for i in range(count)])]
    reduce_sum x3, other arithmetic: 38.3 us -> 1.51 us  [the longest x1 0.7 us: block_places(): total = jnp.sum(used.astype(jnp.int32))]
    convert_element_type x7 -> x0, local copies, waits for them, and re-layouts: 35.4 us -> none  [the longest x4 27.6 us: scan_heads(): gate_rows.astype(jnp.float32)]
    all_to_all x8 -> x2, starting transfers between devices: 32.9 us -> 8.87 us  [spread(): return lax.all_to_all(packed, 'tp', split_axis=0, concat_axis=0, tiled=True)]
  transfers between devices with their start and end apart: 10 -> 19, of which waited for: 1 -> 6; matrix products, arithmetic and copies ran while one was open for 84% -> 9% of each run, Pallas kernels for 0% -> 35%
where the time goes in v1:
time: 141 us; the launch traced here: 140 us
  Pallas kernels  52.8 us (37%)
  waiting for transfers between devices  41.7 us (30%)
  starting transfers between devices  27.2 us (19%)
  local copies, waits for them, and re-layouts  9.64 us (7%)
  other arithmetic  7.31 us (5%)
  between operations  1.81 us (1%)
    ppermute x17, waiting for transfers between devices, swap(): return lax.ppermute(value, axis, [(i, i ^ mask) for i in range(count)])  41.7 us
    ppermute x17, starting transfers between devices, swap(): return lax.ppermute(value, axis, [(i, i ^ mask) for i in range(count)])  18.3 us
    pallas_call x2, Pallas kernels, scan_group(): pl.pallas_call(functools.partial(scan_body, parts, sources, heads, group)...  17.7 us
    pallas_call x1, Pallas kernels, attention(): pl.pallas_call(functools.partial(attention_body, parts, [offsets for _, o...  16.2 us
    all_to_all x2, starting transfers between devices, spread(): return lax.all_to_all(packed, 'tp', split_axis=0, concat_axis=0, tiled=True)  8.87 us
    pallas_call x2, Pallas kernels, norm_group(): pl.pallas_call(functools.partial(norm_body, parts, group, local_groups),...  7.8 us
    pallas_call x1, Pallas kernels, pack(): pl.pallas_call(body, grid=(parts,), in_specs=specs + [pl.BlockSpec(gain.s...  5.14 us
    unnamed x49, local copies, waits for them, and re-layouts  4.25 us
  transfers between devices with their start and end apart: 19, of which 6 were waited for; matrix products, arithmetic and copies ran while one was open for 9% of the time, Pallas kernels for 35%

profile of v1, /device:TPU:0, one launch (start us, length us, event | category | flops | bytes accessed | tf_op | source)
XLA Modules:
  0.0 140.5 jit_solution(3395989203300468288)
XLA Ops:
  0.6 1.0 copy.23
  1.6 4.1 %collective-permute-start = (bf16[4,2,64,256]{3,2,1,0:T(8,128)(2,1)S(1)}, bf16[4,2,64,256]{3,2,1,0:T(8,128)(2,1)S(1)}, u32[]{:S(2)}, u32[]{:S(2)}) collective-permute-start(bf16[4,2,64,256]{3,2,1,0:T(8,128)(2,1)S(1)} %bitcast.48), channel_id=1, source_target_pairs={{0,16},{4,20},{8,24},{12,28},{16,0},{20,4},{24,8},{28,12},{1,17},{... | collective-permute-start | bytes 786440 | tf_op jit(solution)/shard_map/ppermute | solution.py:76
  5.7 1.3 fusion.15
  7.0 1.6 %collective-permute-start.1 = (bf16[1024,256]{1,0:T(8,128)(2,1)S(1)}, bf16[1024,256]{1,0:T(8,128)(2,1)S(1)}, u32[]{:S(2)}, u32[]{:S(2)}) collective-permute-start(bf16[1024,256]{1,0:T(8,128)(2,1)S(1)} %bitcast.45), channel_id=1, source_target_pairs={{0,8},{4,12},{8,0},{12,4},{16,24},{20,28},{24,16},{28,20},{1,9},{5... | collective-permute-start | bytes 1572872 | tf_op jit(solution)/shard_map/ppermute | solution.py:76
  8.7 1.5 %collective-permute-start.2 = (bf16[2048,256]{1,0:T(8,128)(2,1)}, bf16[2048,256]{1,0:T(8,128)(2,1)S(1)}, u32[]{:S(2)}, u32[]{:S(2)}) collective-permute-start(bf16[2048,256]{1,0:T(8,128)(2,1)} %bitcast.21), channel_id=1, source_target_pairs={{0,4},{4,0},{8,12},{12,8},{16,20},{20,16},{24,28},{28,24},{1,5},{5... | collective-permute-start | bytes 3145736 | tf_op jit(solution)/shard_map/ppermute | solution.py:76
  10.2 5.1 %shard_map.176 = bf16[4,128,4864]{2,1,0:T(8,128)(2,1)} custom-call(bf16[128,8192]{1,0:T(8,128)(2,1)} %bitcast.59, bf16[128,4096]{1,0:T(8,128)(2,1)} %bitcast.60, bf16[128,4096]{1,0:T(8,128)(2,1)} %bitcast.61, bf16[128,2048]{1,0:T(8,128)(2,1)} %bitcast.62, bf16[128,128]{1,0:T(8,128)(2,1)} %bitcast.63, f32[16,128]{1,0:T(8,128)} %bitcast.64), custom_call_target="tpu_custom_call" | custom-call | flops 1024 | bytes 1024 | tf_op jit(solution)/shard_map/pallas_call | solution.py:59
  15.4 5.2 %all-to-all-start = ((bf16[4,128,4864]{2,1,0:T(8,128)(2,1)}), bf16[4,128,4864]{2,1,0:T(8,128)(2,1)}, u32[]{:S(2)}, u32[]{:S(2)}) async-start(bf16[4,128,4864]{2,1,0:T(8,128)(2,1)} %shard_map.176), calls=%async_computation | async-start | bytes 9961472 | tf_op jit(solution)/shard_map/all_to_all | solution.py:71
  25.1 0.8 shard_map.177.refs_0_
  28.9 1.8 %collective-permute-start.3 = (bf16[1024,256]{1,0:T(8,128)(2,1)S(1)}, bf16[1024,256]{1,0:T(8,128)(2,1)S(1)}, u32[]{:S(2)}, u32[]{:S(2)}) collective-permute-start(bf16[1024,256]{1,0:T(8,128)(2,1)S(1)} %collective-permute-done.1.refs_1_), channel_id=1, source_target_pairs={{0,4},{4,0},{8,12},{12,8},{16,20},{20,16},{24,28},{28,24},{1,5},{5... | collective-permute-start | bytes 1572872 | tf_op jit(solution)/shard_map/ppermute | solution.py:76
  30.8 1.3 pad_add_fusion.4.where_ref
  33.3 17.7 %collective-permute-done.4.refs_1_ = bf16[8,2,64,256]{3,2,1,0:T(8,128)(2,1)} collective-permute-done((bf16[8,2,64,256]{3,2,1,0:T(8,128)(2,1)}, bf16[8,2,64,256]{3,2,1,0:T(8,128)(2,1)}, u32[]{:S(2)}, u32[]{:S(2)}) %collective-permute-start.4) | collective-permute-done | bytes 524320 | tf_op jit(solution)/shard_map/ppermute | solution.py:76
  51.0 1.5 %collective-permute-start.6 = (bf16[8,2,64,256]{3,2,1,0:T(8,128)(2,1)}, bf16[8,2,64,256]{3,2,1,0:T(8,128)(2,1)}, u32[]{:S(2)}, u32[]{:S(2)}) collective-permute-start(bf16[8,2,64,256]{3,2,1,0:T(8,128)(2,1)} %collective-permute-done.4.refs_1_), channel_id=1, source_target_pairs={{0,4},{4,0},{8,12},{12,8},{16,20},{20,16},{24,28},{28,24},{1,5},{5... | collective-permute-start | bytes 1572872 | tf_op jit(solution)/shard_map/ppermute | solution.py:76
  53.2 4.3 %collective-permute-done.3.refs_3_ = bf16[1024,256]{1,0:T(8,128)(2,1)S(1)} collective-permute-done((bf16[1024,256]{1,0:T(8,128)(2,1)S(1)}, bf16[1024,256]{1,0:T(8,128)(2,1)S(1)}, u32[]{:S(2)}, u32[]{:S(2)}) %collective-permute-start.3) | collective-permute-done | bytes 524320 | tf_op jit(solution)/shard_map/ppermute | solution.py:76
  57.5 1.5 %collective-permute-start.8 = (bf16[1024,256]{1,0:T(8,128)(2,1)S(1)}, bf16[1024,256]{1,0:T(8,128)(2,1)S(1)}, u32[]{:S(2)}, u32[]{:S(2)}) collective-permute-start(bf16[1024,256]{1,0:T(8,128)(2,1)S(1)} %collective-permute-done.7.refs_1_), channel_id=1, source_target_pairs={{0,4},{4,0},{8,12},{12,8},{16,20},{20,16},{24,28},{28,24},{1,5},{5... | collective-permute-start | bytes 1572872 | tf_op jit(solution)/shard_map/ppermute | solution.py:76
  59.0 1.3 pad_add_fusion.3.where_ref
  60.3 1.2 pad_add_fusion.5.where_ref
  62.2 1.6 %shard_map.178 = bf16[1024,256]{1,0:T(8,128)(2,1)} custom-call(s32[1]{0:T(128)} %bitcast.20.index_ref, bf16[1024,256]{1,0:T(8,128)(2,1)S(1)} %bitcast.46, bf16[1024,256]{1,0:T(8,128)(2,1)S(1)} %collective-permute-done.1.refs_1_, bf16[2048,256]{1,0:T(8,128)(2,1)S(1)} %collective-permute-done.2.refs_2_, bf16[1024,256]{1,0:T(8,128)(2,1)S(1)} %collective-permute-done.3.refs_3_), custom_call_target="tpu_custom_call" | custom-call | flops 1024 | bytes 1024 | tf_op jit(solution)/shard_map/pallas_call | solution.py:353
  64.2 14.0 %collective-permute-done.8.refs_3_ = bf16[1024,256]{1,0:T(8,128)(2,1)S(1)} collective-permute-done((bf16[1024,256]{1,0:T(8,128)(2,1)S(1)}, bf16[1024,256]{1,0:T(8,128)(2,1)S(1)}, u32[]{:S(2)}, u32[]{:S(2)}) %collective-permute-start.8) | collective-permute-done | bytes 524320 | tf_op jit(solution)/shard_map/ppermute | solution.py:76
  78.2 0.7 shard_map.180
  79.5 16.2 %shard_map.179 = bf16[4,128,1024]{2,1,0:T(8,128)(2,1)} custom-call(s32[2]{0:T(128)} %pad_add_fusion.4.where_ref, s32[32]{0:T(128)} %copy-done.23, s32[32]{0:T(128)} %convert_reduce_fusion.place_ref, bf16[4,128,4864]{2,1,0:T(8,128)(2,1)} %all-to-all-done.q_ref.refs_8_.refs_9_.refs_10_.refs_11_, bf16[512,4864]{1,0:T(8,128)(2,1)} %bitcast.22.fresh_ref.x_ref.proj_ref.raw_ref, ...), custom_call_target="tpu_custom_call" | custom-call | flops 18400002048 | bytes 1024 | tf_op jit(solution)/shard_map/pallas_call | solution.py:193
  95.7 3.7 %all-to-all-start.1 = ((bf16[4,128,1024]{2,1,0:T(8,128)(2,1)}), bf16[4,128,1024]{2,1,0:T(8,128)(2,1)S(1)}, u32[]{:S(2)}, u32[]{:S(2)}) async-start(bf16[4,128,1024]{2,1,0:T(8,128)(2,1)} %shard_map.179), calls=%async_computation.1 | async-start | bytes 2097152 | tf_op jit(solution)/shard_map/all_to_all | solution.py:71
  99.4 8.8 %shard_map.183 = (bf16[128,1024]{1,0:T(8,128)(2,1)}, bf16[128,1024]{1,0:T(8,128)(2,1)}, bf16[128,1024]{1,0:T(8,128)(2,1)}, bf16[128,1024]{1,0:T(8,128)(2,1)}) custom-call(s32[3]{0:T(128)} %pad_add_fusion.5.where_ref, bf16[512,4864]{1,0:T(8,128)(2,1)} %bitcast.22.fresh_ref.x_ref.proj_ref.raw_ref, bf16[512,4864]{1,0:T(8,128)(2,1)} %bitcast.22.fresh_ref.x_ref.proj_ref.raw_ref, ...), custom_call_target="tpu_custom_call" | custom-call | flops 9200001024 | bytes 1024 | tf_op jit(solution)/shard_map/pallas_call | solution.py:316
  108.6 1.7 %collective-permute-start.15 = (bf16[128,1024]{1,0:T(8,128)(2,1)}, bf16[128,1024]{1,0:T(8,128)(2,1)S(1)}, u32[]{:S(2)}, u32[]{:S(2)}) collective-permute-start(bf16[128,1024]{1,0:T(8,128)(2,1)} %get-tuple-element.88), channel_id=1, source_target_pairs={{0,2},{1,3},{2,0},{3,1},{4,6},{5,7},{6,4},{7,5},{8,10},{9,11},{10,... | collective-permute-start | bytes 786440 | tf_op jit(solution)/shard_map/ppermute | solution.py:76
  110.3 0.8 copy-done.20
  111.1 8.9 %shard_map.181 = (bf16[128,1024]{1,0:T(8,128)(2,1)}, bf16[128,1024]{1,0:T(8,128)(2,1)}, bf16[128,1024]{1,0:T(8,128)(2,1)}, bf16[128,1024]{1,0:T(8,128)(2,1)}) custom-call(s32[3]{0:T(128)} %pad_add_fusion.3.where_ref, bf16[512,4864]{1,0:T(8,128)(2,1)} %bitcast.22.fresh_ref.x_ref.proj_ref.raw_ref, bf16[512,4864]{1,0:T(8,128)(2,1)} %bitcast.22.fresh_ref.x_ref.proj_ref.raw_ref, ...), custom_call_target="tpu_custom_call" | custom-call | flops 9200001024 | bytes 1024 | tf_op jit(solution)/shard_map/pallas_call | solution.py:316
  120.5 1.7 %collective-permute-start.11 = (bf16[128,1024]{1,0:T(8,128)(2,1)}, bf16[128,1024]{1,0:T(8,128)(2,1)S(1)}, u32[]{:S(2)}, u32[]{:S(2)}) collective-permute-start(bf16[128,1024]{1,0:T(8,128)(2,1)} %get-tuple-element.83), channel_id=1, source_target_pairs={{0,2},{1,3},{2,0},{3,1},{4,6},{5,7},{6,4},{7,5},{8,10},{9,11},{10,... | collective-permute-start | bytes 786440 | tf_op jit(solution)/shard_map/ppermute | solution.py:76
  122.2 2.2 %collective-permute-done.16.refs_3_ = bf16[128,1024]{1,0:T(8,128)(2,1)S(1)} collective-permute-done((bf16[128,1024]{1,0:T(8,128)(2,1)}, bf16[128,1024]{1,0:T(8,128)(2,1)S(1)}, u32[]{:S(2)}, u32[]{:S(2)}) %collective-permute-start.16) | collective-permute-done | bytes 262176 | tf_op jit(solution)/shard_map/ppermute | solution.py:76
  125.1 3.9 %shard_map.184.refs_12_ = bf16[128,8192]{1,0:T(8,128)(2,1)} custom-call(s32[2]{0:T(128)} %pad_add_fusion.2.where_ref, bf16[128,1024]{1,0:T(8,128)(2,1)} %get-tuple-element.86.refs_0_, bf16[128,1024]{1,0:T(8,128)(2,1)} %copy-done.8, bf16[128,1024]{1,0:T(8,128)(2,1)} %copy-done.9, bf16[128,1024]{1,0:T(8,128)(2,1)} %copy-done.11, bf16[128,8192]{1,0:T(8,128)(2,1)} %bitcast.50, ...), custom_call_target="tpu_custom_call" | custom-call | flops 3450000896 | bytes 1024 | tf_op jit(solution)/shard_map/pallas_call | solution.py:466
  129.1 1.0 copy-done.7
  130.0 2.8 %shard_map.182 = bf16[128,4096]{1,0:T(8,128)(2,1)} custom-call(s32[2]{0:T(128)} %pad_add_fusion.2.where_ref, bf16[4,128,1024]{2,1,0:T(8,128)(2,1)} %copy-done.7), custom_call_target="tpu_custom_call" | custom-call | flops 2300001024 | bytes 1024 | tf_op jit(solution)/shard_map/pallas_call | solution.py:496
  132.8 2.8 %collective-permute-done.12.refs_3_ = bf16[128,1024]{1,0:T(8,128)(2,1)S(1)} collective-permute-done((bf16[128,1024]{1,0:T(8,128)(2,1)}, bf16[128,1024]{1,0:T(8,128)(2,1)S(1)}, u32[]{:S(2)}, u32[]{:S(2)}) %collective-permute-start.12) | collective-permute-done | bytes 262176 | tf_op jit(solution)/shard_map/ppermute | solution.py:76
  136.4 3.9 %shard_map.185 = bf16[128,8192]{1,0:T(8,128)(2,1)} custom-call(s32[2]{0:T(128)} %pad_add_fusion.2.where_ref, bf16[128,1024]{1,0:T(8,128)(2,1)} %get-tuple-element.79.refs_0_, bf16[128,1024]{1,0:T(8,128)(2,1)} %copy-done.10, bf16[128,1024]{1,0:T(8,128)(2,1)} %copy-done.12, bf16[128,1024]{1,0:T(8,128)(2,1)} %copy-done.13, ...), custom_call_target="tpu_custom_call", output_to_operand_aliasing={{}: (13, {})} | custom-call | flops 3450000896 | bytes 1024 | tf_op jit(solution)/shard_map/pallas_call | solution.py:466
  (100 shorter events, 12.6 us)
Async XLA Ops:
  1.6 23.5 %collective-permute-start = (bf16[4,2,64,256]{3,2,1,0:T(8,128)(2,1)S(1)}, bf16[4,2,64,256]{3,2,1,0:T(8,128)(2,1)S(1)}, u32[]{:S(2)}, u32[]{:S(2)}) collective-permute-start(bf16[4,2,64,256]{3,2,1,0:T(8,128)(2,1)S(1)} %bitcast.48), channel_id=1, source_target_pairs={{0,16},{4,20},{8,24},{12,28},{16,0},{20,4},{24,8},{28,12},{1,17},{... | collective-permute-start | bytes 786440 | tf_op jit(solution)/shard_map/ppermute | solution.py:76
  7.0 55.2 %copy-start.2 = (bf16[1,16,64,256]{3,2,1,0:T(8,128)(2,1)}, bf16[1,16,64,256]{3,2,1,0:T(8,128)(2,1)S(1)}, u32[]{:S(2)}) copy-start(bf16[1,16,64,256]{3,2,1,0:T(8,128)(2,1)S(1)} %get-tuple-element.90) | copy-start | bytes 1572868
  7.0 71.2 %copy-start.1 = (bf16[1,16,64,256]{3,2,1,0:T(8,128)(2,1)}, bf16[1,16,64,256]{3,2,1,0:T(8,128)(2,1)S(1)}, u32[]{:S(2)}) copy-start(bf16[1,16,64,256]{3,2,1,0:T(8,128)(2,1)S(1)} %get-tuple-element.91) | copy-start | bytes 1572868
  7.0 21.9 %collective-permute-start.1 = (bf16[1024,256]{1,0:T(8,128)(2,1)S(1)}, bf16[1024,256]{1,0:T(8,128)(2,1)S(1)}, u32[]{:S(2)}, u32[]{:S(2)}) collective-permute-start(bf16[1024,256]{1,0:T(8,128)(2,1)S(1)} %bitcast.45), channel_id=1, source_target_pairs={{0,8},{4,12},{8,0},{12,4},{16,24},{20,28},{24,16},{28,20},{1,9},{5... | collective-permute-start | bytes 1572872 | tf_op jit(solution)/shard_map/ppermute | solution.py:76
  8.7 42.3 %collective-permute-start.2 = (bf16[2048,256]{1,0:T(8,128)(2,1)}, bf16[2048,256]{1,0:T(8,128)(2,1)S(1)}, u32[]{:S(2)}, u32[]{:S(2)}) collective-permute-start(bf16[2048,256]{1,0:T(8,128)(2,1)} %bitcast.21), channel_id=1, source_target_pairs={{0,4},{4,0},{8,12},{12,8},{16,20},{20,16},{24,28},{28,24},{1,5},{5... | collective-permute-start | bytes 3145736 | tf_op jit(solution)/shard_map/ppermute | solution.py:76
  15.3 5.2 %copy-start.21 = (s32[8]{0:T(128)S(1)}, s32[8]{0:T(128)}, u32[]{:S(2)}) copy-start(s32[8]{0:T(128)} %param.41) | copy-start | bytes 100
  15.3 5.9 %copy-start.22 = (s32[8]{0:T(128)S(1)}, s32[8]{0:T(128)}, u32[]{:S(2)}) copy-start(s32[8]{0:T(128)} %param.39) | copy-start | bytes 100
  15.4 7.1 %copy-start.16 = (f32[32]{0:T(128)S(1)}, f32[32]{0:T(128)}, u32[]{:S(2)}) copy-start(f32[32]{0:T(128)} %param.33) | copy-start | bytes 388
  15.4 7.2 %copy-start.17 = (f32[32]{0:T(128)S(1)}, f32[32]{0:T(128)}, u32[]{:S(2)}) copy-start(f32[32]{0:T(128)} %param.34) | copy-start | bytes 388
  15.4 8.6 %copy-start.18 = (f32[32]{0:T(128)S(1)}, f32[32]{0:T(128)}, u32[]{:S(2)}) copy-start(f32[32]{0:T(128)} %param.35) | copy-start | bytes 388
  15.4 64.1 %all-to-all-start = ((bf16[4,128,4864]{2,1,0:T(8,128)(2,1)}), bf16[4,128,4864]{2,1,0:T(8,128)(2,1)}, u32[]{:S(2)}, u32[]{:S(2)}) async-start(bf16[4,128,4864]{2,1,0:T(8,128)(2,1)} %shard_map.176), calls=%async_computation | async-start | bytes 9961472 | tf_op jit(solution)/shard_map/all_to_all | solution.py:71
  26.1 26.4 %collective-permute-start.5 = (bf16[8,2,64,256]{3,2,1,0:T(8,128)(2,1)}, bf16[8,2,64,256]{3,2,1,0:T(8,128)(2,1)}, u32[]{:S(2)}, u32[]{:S(2)}) collective-permute-start(bf16[8,2,64,256]{3,2,1,0:T(8,128)(2,1)} %shard_map.177.refs_0_), channel_id=1, source_target_pairs={{0,4},{4,0},{8,12},{12,8},{16,20},{20,16},{24,28},{28,24},{1,5},{5... | collective-permute-start | bytes 1572872 | tf_op jit(solution)/shard_map/ppermute | solution.py:76
  26.7 24.3 %collective-permute-start.4 = (bf16[8,2,64,256]{3,2,1,0:T(8,128)(2,1)}, bf16[8,2,64,256]{3,2,1,0:T(8,128)(2,1)}, u32[]{:S(2)}, u32[]{:S(2)}) collective-permute-start(bf16[8,2,64,256]{3,2,1,0:T(8,128)(2,1)} %shard_map.177.refs_0_), channel_id=1, source_target_pairs={{0,8},{4,12},{8,0},{12,4},{16,24},{20,28},{24,16},{28,20},{1,9},{5... | collective-permute-start | bytes 1572872 | tf_op jit(solution)/shard_map/ppermute | solution.py:76
  27.3 25.9 %collective-permute-start.7 = (bf16[1024,256]{1,0:T(8,128)(2,1)S(1)}, bf16[1024,256]{1,0:T(8,128)(2,1)S(1)}, u32[]{:S(2)}, u32[]{:S(2)}) collective-permute-start(bf16[1024,256]{1,0:T(8,128)(2,1)S(1)} %bitcast.42), channel_id=1, source_target_pairs={{0,16},{4,20},{8,24},{12,28},{16,0},{20,4},{24,8},{28,12},{1,17},{... | collective-permute-start | bytes 1572872 | tf_op jit(solution)/shard_map/ppermute | solution.py:76
  28.2 50.7 %copy-start.23 = (s32[32]{0:T(128)}, s32[32]{0:T(128)S(1)}, u32[]{:S(2)}) copy-start(s32[32]{0:T(128)S(1)} %convert_reduce_fusion.1.often_ref) | copy-start | bytes 388
  28.9 50.0 %copy-start.3 = (bf16[1024,256]{1,0:T(8,128)(2,1)}, bf16[1024,256]{1,0:T(8,128)(2,1)S(1)}, u32[]{:S(2)}) copy-start(bf16[1024,256]{1,0:T(8,128)(2,1)S(1)} %collective-permute-done.1.refs_1_) | copy-start | bytes 1572868
  28.9 28.5 %collective-permute-start.3 = (bf16[1024,256]{1,0:T(8,128)(2,1)S(1)}, bf16[1024,256]{1,0:T(8,128)(2,1)S(1)}, u32[]{:S(2)}, u32[]{:S(2)}) collective-permute-start(bf16[1024,256]{1,0:T(8,128)(2,1)S(1)} %collective-permute-done.1.refs_1_), channel_id=1, source_target_pairs={{0,4},{4,0},{8,12},{12,8},{16,20},{20,16},{24,28},{28,24},{1,5},{5... | collective-permute-start | bytes 1572872 | tf_op jit(solution)/shard_map/ppermute | solution.py:76
  51.0 28.0 %copy-start = (bf16[2048,256]{1,0:T(8,128)(2,1)}, bf16[2048,256]{1,0:T(8,128)(2,1)S(1)}, u32[]{:S(2)}) copy-start(bf16[2048,256]{1,0:T(8,128)(2,1)S(1)} %collective-permute-done.2.refs_2_) | copy-start | bytes 3145732
  51.0 28.5 %collective-permute-start.6 = (bf16[8,2,64,256]{3,2,1,0:T(8,128)(2,1)}, bf16[8,2,64,256]{3,2,1,0:T(8,128)(2,1)}, u32[]{:S(2)}, u32[]{:S(2)}) collective-permute-start(bf16[8,2,64,256]{3,2,1,0:T(8,128)(2,1)} %collective-permute-done.4.refs_1_), channel_id=1, source_target_pairs={{0,4},{4,0},{8,12},{12,8},{16,20},{20,16},{24,28},{28,24},{1,5},{5... | collective-permute-start | bytes 1572872 | tf_op jit(solution)/shard_map/ppermute | solution.py:76
  53.2 25.8 %copy-start.4 = (bf16[1024,256]{1,0:T(8,128)(2,1)}, bf16[1024,256]{1,0:T(8,128)(2,1)S(1)}, u32[]{:S(2)}) copy-start(bf16[1024,256]{1,0:T(8,128)(2,1)S(1)} %collective-permute-done.7.refs_1_) | copy-start | bytes 1572868
  57.5 21.5 %copy-start.5 = (bf16[1024,256]{1,0:T(8,128)(2,1)}, bf16[1024,256]{1,0:T(8,128)(2,1)S(1)}, u32[]{:S(2)}) copy-start(bf16[1024,256]{1,0:T(8,128)(2,1)S(1)} %collective-permute-done.3.refs_3_) | copy-start | bytes 1572868
  57.5 20.7 %collective-permute-start.8 = (bf16[1024,256]{1,0:T(8,128)(2,1)S(1)}, bf16[1024,256]{1,0:T(8,128)(2,1)S(1)}, u32[]{:S(2)}, u32[]{:S(2)}) collective-permute-start(bf16[1024,256]{1,0:T(8,128)(2,1)S(1)} %collective-permute-done.7.refs_1_), channel_id=1, source_target_pairs={{0,4},{4,0},{8,12},{12,8},{16,20},{20,16},{24,28},{28,24},{1,5},{5... | collective-permute-start | bytes 1572872 | tf_op jit(solution)/shard_map/ppermute | solution.py:76
  63.8 35.7 %collective-permute-start.13 = (bf16[1024,256]{1,0:T(8,128)(2,1)}, bf16[1024,256]{1,0:T(8,128)(2,1)}, u32[]{:S(2)}, u32[]{:S(2)}) collective-permute-start(bf16[1024,256]{1,0:T(8,128)(2,1)} %shard_map.178), channel_id=1, source_target_pairs={{0,16},{4,20},{8,24},{12,28},{16,0},{20,4},{24,8},{28,12},{1,17},{... | collective-permute-start | bytes 1572872 | tf_op jit(solution)/shard_map/ppermute | solution.py:76
  79.0 31.3 %collective-permute-start.9 = (bf16[1024,256]{1,0:T(8,128)(2,1)S(1)}, bf16[1024,256]{1,0:T(8,128)(2,1)S(1)}, u32[]{:S(2)}, u32[]{:S(2)}) collective-permute-start(bf16[1024,256]{1,0:T(8,128)(2,1)S(1)} %shard_map.180), channel_id=1, source_target_pairs={{0,8},{4,12},{8,0},{12,4},{16,24},{20,28},{24,16},{28,20},{1,9},{5... | collective-permute-start | bytes 1572872 | tf_op jit(solution)/shard_map/ppermute | solution.py:76
  95.7 33.3 %all-to-all-start.1 = ((bf16[4,128,1024]{2,1,0:T(8,128)(2,1)}), bf16[4,128,1024]{2,1,0:T(8,128)(2,1)S(1)}, u32[]{:S(2)}, u32[]{:S(2)}) async-start(bf16[4,128,1024]{2,1,0:T(8,128)(2,1)} %shard_map.179), calls=%async_computation.1 | async-start | bytes 2097152 | tf_op jit(solution)/shard_map/all_to_all | solution.py:71
  108.3 13.9 %collective-permute-start.14 = (bf16[128,1024]{1,0:T(8,128)(2,1)}, bf16[128,1024]{1,0:T(8,128)(2,1)S(1)}, u32[]{:S(2)}, u32[]{:S(2)}) collective-permute-start(bf16[128,1024]{1,0:T(8,128)(2,1)} %get-tuple-element.87), channel_id=1, source_target_pairs={{0,1},{1,0},{2,3},{3,2},{4,5},{5,4},{6,7},{7,6},{8,9},{9,8},{10,11... | collective-permute-start | bytes 786440 | tf_op jit(solution)/shard_map/ppermute | solution.py:76
  108.6 13.6 %collective-permute-start.15 = (bf16[128,1024]{1,0:T(8,128)(2,1)}, bf16[128,1024]{1,0:T(8,128)(2,1)S(1)}, u32[]{:S(2)}, u32[]{:S(2)}) collective-permute-start(bf16[128,1024]{1,0:T(8,128)(2,1)} %get-tuple-element.88), channel_id=1, source_target_pairs={{0,2},{1,3},{2,0},{3,1},{4,6},{5,7},{6,4},{7,5},{8,10},{9,11},{10,... | collective-permute-start | bytes 786440 | tf_op jit(solution)/shard_map/ppermute | solution.py:76
  110.3 14.1 %collective-permute-start.16 = (bf16[128,1024]{1,0:T(8,128)(2,1)}, bf16[128,1024]{1,0:T(8,128)(2,1)S(1)}, u32[]{:S(2)}, u32[]{:S(2)}) collective-permute-start(bf16[128,1024]{1,0:T(8,128)(2,1)} %get-tuple-element.89), channel_id=1, source_target_pairs={{0,3},{1,2},{2,1},{3,0},{4,7},{5,6},{6,5},{7,4},{8,11},{9,10},{10,... | collective-permute-start | bytes 786440 | tf_op jit(solution)/shard_map/ppermute | solution.py:76
  120.0 12.8 %collective-permute-start.10 = (bf16[128,1024]{1,0:T(8,128)(2,1)}, bf16[128,1024]{1,0:T(8,128)(2,1)S(1)}, u32[]{:S(2)}, u32[]{:S(2)}) collective-permute-start(bf16[128,1024]{1,0:T(8,128)(2,1)} %get-tuple-element.82), channel_id=1, source_target_pairs={{0,1},{1,0},{2,3},{3,2},{4,5},{5,4},{6,7},{7,6},{8,9},{9,8},{10,11... | collective-permute-start | bytes 786440 | tf_op jit(solution)/shard_map/ppermute | solution.py:76
  120.5 12.3 %collective-permute-start.11 = (bf16[128,1024]{1,0:T(8,128)(2,1)}, bf16[128,1024]{1,0:T(8,128)(2,1)S(1)}, u32[]{:S(2)}, u32[]{:S(2)}) collective-permute-start(bf16[128,1024]{1,0:T(8,128)(2,1)} %get-tuple-element.83), channel_id=1, source_target_pairs={{0,2},{1,3},{2,0},{3,1},{4,6},{5,7},{6,4},{7,5},{8,10},{9,11},{10,... | collective-permute-start | bytes 786440 | tf_op jit(solution)/shard_map/ppermute | solution.py:76
  122.2 13.5 %collective-permute-start.12 = (bf16[128,1024]{1,0:T(8,128)(2,1)}, bf16[128,1024]{1,0:T(8,128)(2,1)S(1)}, u32[]{:S(2)}, u32[]{:S(2)}) collective-permute-start(bf16[128,1024]{1,0:T(8,128)(2,1)} %get-tuple-element.84), channel_id=1, source_target_pairs={{0,3},{1,2},{2,1},{3,0},{4,7},{5,6},{6,5},{7,4},{8,11},{9,10},{10,... | collective-permute-start | bytes 786440 | tf_op jit(solution)/shard_map/ppermute | solution.py:76
  132.8 2.9 %copy-start.10 = (bf16[128,1024]{1,0:T(8,128)(2,1)}, bf16[128,1024]{1,0:T(8,128)(2,1)S(1)}, u32[]{:S(2)}) copy-start(bf16[128,1024]{1,0:T(8,128)(2,1)S(1)} %collective-permute-done.10.refs_1_) | copy-start | bytes 786436
  (11 other events, 15.9 us)

commit v2 on v1

--- a/solution.py
+++ b/solution.py
@@ -376,7 +376,7 @@
     return sum(jnp.where(distance == offset, i, 0) for i, offset in enumerate(offsets))
 
 
-def fetch_state(own, far, far_mask, entries, order, gate, late_gate, group):
+def fetch_state(own, far, far_mask, entries, order, gate, late_gate, last_gate, group):
     count = lax.axis_size("req")
     size = own.shape[0]
     offsets, held = [0], [own]
@@ -398,7 +398,7 @@
     source = jnp.where((distance & last) == 0, slot_of(distance, offsets), len(held))
     choices = jnp.stack([slot_of(flipped ^ every, offsets), source]).astype(jnp.int32)
     mine = lax.dynamic_slice_in_dim(choices, lax.axis_index("req"), 1, axis=1)[:, 0]
-    begun = choose(mine[0:1], held, group, size)
+    begun = choose(after(mine[0:1], *last_gate), held, group, size)
     return mine[1], held + [swap(begun, "req", last)], begun
 
 
@@ -574,24 +574,28 @@
         pools += moved
 
     entries = after(state_entry, pool_held)
-    state_lists, begun, late_gate = [None] * local_groups, [], [array for array, _ in pools[1:3]]
-    for group in reversed(range(local_groups)):
-        gates = ([pool_far], late_gate) if group % 2 == 0 else ([], [])
+    state_lists, begun = [None] * local_groups, []
+
+    def fetch(group, last_gate):
+        gates = ([pools[1][0]], [pools[2][0]]) if group % 2 == 0 else ([], [])
         source, values, sent = fetch_state(
-            state_groups[group], state_far, far_mask, entries, bit_order(owners, group), *gates, group
+            state_groups[group], state_far, far_mask, entries, bit_order(owners, group), *gates, last_gate, group
         )
         state_lists[group] = (source, values)
         begun.append(sent)
-        late_gate = late_gate + [values[-2]]
+
+    for group in reversed(range(1, local_groups)):
+        fetch(group, [])
 
     targets = after(block_owner, pool_held)[request] * pool_local + block_slot[request]
     often, place, total = block_places(targets, block_count[request], pool_total)
     where = jnp.stack([request, total]).astype(jnp.int32)
     live = jnp.stack([share, suffix_len[request] - share * rows]).astype(jnp.int32)
 
-    where = after(where, *begun[:-1])
+    where = after(where, *begun)
     mixed = attention(joined, pools, where, often, place, listed, q_column, q_width)
     attn_back = spread(mixed)
+    fetch(0, [mixed])
 
     ssm_out = None
     skips = jnp.repeat(skip_gain, channels)[None, :]
@@ -604,7 +608,7 @@
         shift = lax.rem(head_total - start, head_total)
         cols = slice(group * group_width, (group + 1) * group_width)
         source, values = state_lists[group]
-        where = after(jnp.stack([share, shift, source]).astype(jnp.int32), mixed)
+        where = after(jnp.stack([share, shift, source]).astype(jnp.int32), mixed, begun[-1])
         scanned = scan_group(
             joined, step_column, values, where, head_rows, skips[:, cols], heads, group, local_groups
         )

time: 141 us -> 144 us (1.021)
  waiting for transfers between devices: 41.7 us -> 45.4 us
    ppermute x17, waiting for transfers between devices: 41.7 us -> 45.4 us  [swap(): return lax.ppermute(value, axis, [(i, i ^ mask) for i in range(count)])]
    unnamed x49 -> x47, local copies, waits for them, and re-layouts: 4.25 us -> 3.34 us
  transfers between devices with their start and end apart: 19 -> 19, of which waited for: 6 -> 5; matrix products, arithmetic and copies ran while one was open for 9% -> 9% of each run, Pallas kernels for 35% -> 34%
where the time goes in v2:
time: 144 us; the launch traced here: 143 us
  Pallas kernels  52.9 us (37%)
  waiting for transfers between devices  45.4 us (32%)
  starting transfers between devices  27.2 us (19%)
  local copies, waits for them, and re-layouts  8.7 us (6%)
  other arithmetic  7.33 us (5%)
  between operations  1.74 us (1%)
    ppermute x17, waiting for transfers between devices, swap(): return lax.ppermute(value, axis, [(i, i ^ mask) for i in range(count)])  45.4 us
    pallas_call x2, Pallas kernels, scan_group(): pl.pallas_call(functools.partial(scan_body, parts, sources, heads, group)...  17.8 us
    ppermute x17, starting transfers between devices, swap(): return lax.ppermute(value, axis, [(i, i ^ mask) for i in range(count)])  17.8 us
    pallas_call x1, Pallas kernels, attention(): pl.pallas_call(functools.partial(attention_body, parts, [offsets for _, o...  16.2 us
    all_to_all x2, starting transfers between devices, spread(): return lax.all_to_all(packed, 'tp', split_axis=0, concat_axis=0, tiled=True)  9.41 us
    pallas_call x2, Pallas kernels, norm_group(): pl.pallas_call(functools.partial(norm_body, parts, group, local_groups),...  7.8 us
    pallas_call x1, Pallas kernels, pack(): pl.pallas_call(body, grid=(parts,), in_specs=specs + [pl.BlockSpec(gain.s...  5.12 us
    unnamed x47, local copies, waits for them, and re-layouts  3.34 us
  transfers between devices with their start and end apart: 19, of which 5 were waited for; matrix products, arithmetic and copies ran while one was open for 9% of the time, Pallas kernels for 34%

profile of v2, /device:TPU:0, one launch (start us, length us, event | category | flops | bytes accessed | tf_op | source)
XLA Modules:
  0.0 143.3 jit_solution(10797379543563478881)
XLA Ops:
  0.6 1.0 copy.23
  1.6 4.1 %collective-permute-start = (bf16[4,2,64,256]{3,2,1,0:T(8,128)(2,1)S(1)}, bf16[4,2,64,256]{3,2,1,0:T(8,128)(2,1)S(1)}, u32[]{:S(2)}, u32[]{:S(2)}) collective-permute-start(bf16[4,2,64,256]{3,2,1,0:T(8,128)(2,1)S(1)} %bitcast.48), channel_id=1, source_target_pairs={{0,16},{4,20},{8,24},{12,28},{16,0},{20,4},{24,8},{28,12},{1,17},{... | collective-permute-start | bytes 786440 | tf_op jit(solution)/shard_map/ppermute | solution.py:76
  5.7 1.3 fusion.15
  7.0 1.6 %collective-permute-start.1 = (bf16[1024,256]{1,0:T(8,128)(2,1)S(1)}, bf16[1024,256]{1,0:T(8,128)(2,1)S(1)}, u32[]{:S(2)}, u32[]{:S(2)}) collective-permute-start(bf16[1024,256]{1,0:T(8,128)(2,1)S(1)} %bitcast.45), channel_id=1, source_target_pairs={{0,8},{4,12},{8,0},{12,4},{16,24},{20,28},{24,16},{28,20},{1,9},{5... | collective-permute-start | bytes 1572872 | tf_op jit(solution)/shard_map/ppermute | solution.py:76
  8.7 1.5 %collective-permute-start.2 = (bf16[2048,256]{1,0:T(8,128)(2,1)}, bf16[2048,256]{1,0:T(8,128)(2,1)S(1)}, u32[]{:S(2)}, u32[]{:S(2)}) collective-permute-start(bf16[2048,256]{1,0:T(8,128)(2,1)} %bitcast.21), channel_id=1, source_target_pairs={{0,4},{4,0},{8,12},{12,8},{16,20},{20,16},{24,28},{28,24},{1,5},{5... | collective-permute-start | bytes 3145736 | tf_op jit(solution)/shard_map/ppermute | solution.py:76
  10.2 5.1 %shard_map.176 = bf16[4,128,4864]{2,1,0:T(8,128)(2,1)} custom-call(bf16[128,8192]{1,0:T(8,128)(2,1)} %bitcast.59, bf16[128,4096]{1,0:T(8,128)(2,1)} %bitcast.60, bf16[128,4096]{1,0:T(8,128)(2,1)} %bitcast.61, bf16[128,2048]{1,0:T(8,128)(2,1)} %bitcast.62, bf16[128,128]{1,0:T(8,128)(2,1)} %bitcast.63, f32[16,128]{1,0:T(8,128)} %bitcast.64), custom_call_target="tpu_custom_call" | custom-call | flops 1024 | bytes 1024 | tf_op jit(solution)/shard_map/pallas_call | solution.py:59
  15.4 5.2 %all-to-all-start = ((bf16[4,128,4864]{2,1,0:T(8,128)(2,1)}), bf16[4,128,4864]{2,1,0:T(8,128)(2,1)}, u32[]{:S(2)}, u32[]{:S(2)}) async-start(bf16[4,128,4864]{2,1,0:T(8,128)(2,1)} %shard_map.176), calls=%async_computation | async-start | bytes 9961472 | tf_op jit(solution)/shard_map/all_to_all | solution.py:71
  25.0 0.8 shard_map.177.refs_0_
  27.8 0.7 fusion.14
  29.4 1.3 pad_add_fusion.4.where_ref
  31.3 1.5 %collective-permute-start.3 = (bf16[1024,256]{1,0:T(8,128)(2,1)S(1)}, bf16[1024,256]{1,0:T(8,128)(2,1)S(1)}, u32[]{:S(2)}, u32[]{:S(2)}) collective-permute-start(bf16[1024,256]{1,0:T(8,128)(2,1)S(1)} %collective-permute-done.1.refs_1_), channel_id=1, source_target_pairs={{0,4},{4,0},{8,12},{12,8},{16,20},{20,16},{24,28},{28,24},{1,5},{5... | collective-permute-start | bytes 1572872 | tf_op jit(solution)/shard_map/ppermute | solution.py:76
  32.8 8.0 %collective-permute-done.4.refs_1_ = bf16[8,2,64,256]{3,2,1,0:T(8,128)(2,1)} collective-permute-done((bf16[8,2,64,256]{3,2,1,0:T(8,128)(2,1)}, bf16[8,2,64,256]{3,2,1,0:T(8,128)(2,1)}, u32[]{:S(2)}, u32[]{:S(2)}) %collective-permute-start.4) | collective-permute-done | bytes 524320 | tf_op jit(solution)/shard_map/ppermute | solution.py:76
  41.2 1.5 %collective-permute-start.6 = (bf16[8,2,64,256]{3,2,1,0:T(8,128)(2,1)}, bf16[8,2,64,256]{3,2,1,0:T(8,128)(2,1)}, u32[]{:S(2)}, u32[]{:S(2)}) collective-permute-start(bf16[8,2,64,256]{3,2,1,0:T(8,128)(2,1)} %collective-permute-done.4.refs_1_), channel_id=1, source_target_pairs={{0,4},{4,0},{8,12},{12,8},{16,20},{20,16},{24,28},{28,24},{1,5},{5... | collective-permute-start | bytes 1572872 | tf_op jit(solution)/shard_map/ppermute | solution.py:76
  42.7 1.3 pad_add_fusion.3.where_ref
  44.0 1.3 pad_add_fusion.5.where_ref
  45.9 11.6 %collective-permute-done.3.refs_3_ = bf16[1024,256]{1,0:T(8,128)(2,1)S(1)} collective-permute-done((bf16[1024,256]{1,0:T(8,128)(2,1)S(1)}, bf16[1024,256]{1,0:T(8,128)(2,1)S(1)}, u32[]{:S(2)}, u32[]{:S(2)}) %collective-permute-start.3) | collective-permute-done | bytes 524320 | tf_op jit(solution)/shard_map/ppermute | solution.py:76
  57.5 1.5 %shard_map.178 = bf16[1024,256]{1,0:T(8,128)(2,1)} custom-call(s32[1]{0:T(128)} %bitcast.20.index_ref, bf16[1024,256]{1,0:T(8,128)(2,1)S(1)} %bitcast.46, bf16[1024,256]{1,0:T(8,128)(2,1)S(1)} %collective-permute-done.1.refs_1_, bf16[2048,256]{1,0:T(8,128)(2,1)S(1)} %collective-permute-done.2.refs_2_, bf16[1024,256]{1,0:T(8,128)(2,1)S(1)} %collective-permute-done.3.refs_3_), custom_call_target="tpu_custom_call" | custom-call | flops 1024 | bytes 1024 | tf_op jit(solution)/shard_map/pallas_call | solution.py:353
  59.4 17.9 %collective-permute-done.7.refs_1_ = bf16[1024,256]{1,0:T(8,128)(2,1)S(1)} collective-permute-done((bf16[1024,256]{1,0:T(8,128)(2,1)S(1)}, bf16[1024,256]{1,0:T(8,128)(2,1)S(1)}, u32[]{:S(2)}, u32[]{:S(2)}) %collective-permute-start.7) | collective-permute-done | bytes 524320 | tf_op jit(solution)/shard_map/ppermute | solution.py:76
  77.3 1.5 %collective-permute-start.8 = (bf16[1024,256]{1,0:T(8,128)(2,1)S(1)}, bf16[1024,256]{1,0:T(8,128)(2,1)S(1)}, u32[]{:S(2)}, u32[]{:S(2)}) collective-permute-start(bf16[1024,256]{1,0:T(8,128)(2,1)S(1)} %collective-permute-done.7.refs_1_), channel_id=1, source_target_pairs={{0,4},{4,0},{8,12},{12,8},{16,20},{20,16},{24,28},{28,24},{1,5},{5... | collective-permute-start | bytes 1572872 | tf_op jit(solution)/shard_map/ppermute | solution.py:76
  78.9 16.2 %shard_map.179 = bf16[4,128,1024]{2,1,0:T(8,128)(2,1)} custom-call(s32[2]{0:T(128)} %pad_add_fusion.4.where_ref, s32[32]{0:T(128)} %copy-done.22, s32[32]{0:T(128)} %convert_reduce_fusion.place_ref, bf16[4,128,4864]{2,1,0:T(8,128)(2,1)} %all-to-all-done.q_ref.refs_8_.refs_9_.refs_10_.refs_11_, bf16[512,4864]{1,0:T(8,128)(2,1)} %bitcast.22.fresh_ref.x_ref.proj_ref.raw_ref, ...), custom_call_target="tpu_custom_call" | custom-call | flops 18400002048 | bytes 1024 | tf_op jit(solution)/shard_map/pallas_call | solution.py:193
  95.1 4.3 %all-to-all-start.1 = ((bf16[4,128,1024]{2,1,0:T(8,128)(2,1)}), bf16[4,128,1024]{2,1,0:T(8,128)(2,1)}, u32[]{:S(2)}, u32[]{:S(2)}) async-start(bf16[4,128,1024]{2,1,0:T(8,128)(2,1)} %shard_map.179), calls=%async_computation.1 | async-start | bytes 2097152 | tf_op jit(solution)/shard_map/all_to_all | solution.py:71
  99.4 0.9 shard_map.180
  100.4 8.9 %shard_map.183 = (bf16[128,1024]{1,0:T(8,128)(2,1)}, bf16[128,1024]{1,0:T(8,128)(2,1)}, bf16[128,1024]{1,0:T(8,128)(2,1)}, bf16[128,1024]{1,0:T(8,128)(2,1)}) custom-call(s32[3]{0:T(128)} %pad_add_fusion.5.where_ref, bf16[512,4864]{1,0:T(8,128)(2,1)} %bitcast.22.fresh_ref.x_ref.proj_ref.raw_ref, bf16[512,4864]{1,0:T(8,128)(2,1)} %bitcast.22.fresh_ref.x_ref.proj_ref.raw_ref, ...), custom_call_target="tpu_custom_call" | custom-call | flops 9200001024 | bytes 1024 | tf_op jit(solution)/shard_map/pallas_call | solution.py:316
  109.8 1.7 %collective-permute-start.15 = (bf16[128,1024]{1,0:T(8,128)(2,1)}, bf16[128,1024]{1,0:T(8,128)(2,1)S(1)}, u32[]{:S(2)}, u32[]{:S(2)}) collective-permute-start(bf16[128,1024]{1,0:T(8,128)(2,1)} %get-tuple-element.90), channel_id=1, source_target_pairs={{0,2},{1,3},{2,0},{3,1},{4,6},{5,7},{6,4},{7,5},{8,10},{9,11},{10,... | collective-permute-start | bytes 786440 | tf_op jit(solution)/shard_map/ppermute | solution.py:76
  111.5 3.1 %collective-permute-done.9.refs_4_ = bf16[1024,256]{1,0:T(8,128)(2,1)S(1)} collective-permute-done((bf16[1024,256]{1,0:T(8,128)(2,1)S(1)}, bf16[1024,256]{1,0:T(8,128)(2,1)S(1)}, u32[]{:S(2)}, u32[]{:S(2)}) %collective-permute-start.9) | collective-permute-done | bytes 524320 | tf_op jit(solution)/shard_map/ppermute | solution.py:76
  114.6 0.8 copy-done.19
  115.4 8.9 %shard_map.181 = (bf16[128,1024]{1,0:T(8,128)(2,1)}, bf16[128,1024]{1,0:T(8,128)(2,1)}, bf16[128,1024]{1,0:T(8,128)(2,1)}, bf16[128,1024]{1,0:T(8,128)(2,1)}) custom-call(s32[3]{0:T(128)} %pad_add_fusion.3.where_ref, bf16[512,4864]{1,0:T(8,128)(2,1)} %bitcast.22.fresh_ref.x_ref.proj_ref.raw_ref, bf16[512,4864]{1,0:T(8,128)(2,1)} %bitcast.22.fresh_ref.x_ref.proj_ref.raw_ref, ...), custom_call_target="tpu_custom_call" | custom-call | flops 9200001024 | bytes 1024 | tf_op jit(solution)/shard_map/pallas_call | solution.py:316
  124.4 1.7 %collective-permute-start.11 = (bf16[128,1024]{1,0:T(8,128)(2,1)}, bf16[128,1024]{1,0:T(8,128)(2,1)S(1)}, u32[]{:S(2)}, u32[]{:S(2)}) collective-permute-start(bf16[128,1024]{1,0:T(8,128)(2,1)} %get-tuple-element.85), channel_id=1, source_target_pairs={{0,2},{1,3},{2,0},{3,1},{4,6},{5,7},{6,4},{7,5},{8,10},{9,11},{10,... | collective-permute-start | bytes 786440 | tf_op jit(solution)/shard_map/ppermute | solution.py:76
  127.1 3.9 %shard_map.184.refs_12_ = bf16[128,8192]{1,0:T(8,128)(2,1)} custom-call(s32[2]{0:T(128)} %pad_add_fusion.2.where_ref, bf16[128,1024]{1,0:T(8,128)(2,1)} %get-tuple-element.88.refs_0_, bf16[128,1024]{1,0:T(8,128)(2,1)} %copy-done.7, bf16[128,1024]{1,0:T(8,128)(2,1)} %copy-done.8, bf16[128,1024]{1,0:T(8,128)(2,1)} %copy-done.10, bf16[128,8192]{1,0:T(8,128)(2,1)} %bitcast.50, ...), custom_call_target="tpu_custom_call" | custom-call | flops 3450000896 | bytes 1024 | tf_op jit(solution)/shard_map/pallas_call | solution.py:466
  131.0 2.8 %shard_map.182 = bf16[128,4096]{1,0:T(8,128)(2,1)} custom-call(s32[2]{0:T(128)} %pad_add_fusion.2.where_ref, bf16[4,128,1024]{2,1,0:T(8,128)(2,1)} %all-to-all-done.1.in_ref), custom_call_target="tpu_custom_call" | custom-call | flops 2300001024 | bytes 1024 | tf_op jit(solution)/shard_map/pallas_call | solution.py:496
  133.8 4.7 %collective-permute-done.12.refs_3_ = bf16[128,1024]{1,0:T(8,128)(2,1)S(1)} collective-permute-done((bf16[128,1024]{1,0:T(8,128)(2,1)}, bf16[128,1024]{1,0:T(8,128)(2,1)S(1)}, u32[]{:S(2)}, u32[]{:S(2)}) %collective-permute-start.12) | collective-permute-done | bytes 262176 | tf_op jit(solution)/shard_map/ppermute | solution.py:76
  139.2 3.9 %shard_map.185 = bf16[128,8192]{1,0:T(8,128)(2,1)} custom-call(s32[2]{0:T(128)} %pad_add_fusion.2.where_ref, bf16[128,1024]{1,0:T(8,128)(2,1)} %get-tuple-element.81.refs_0_, bf16[128,1024]{1,0:T(8,128)(2,1)} %copy-done.9, bf16[128,1024]{1,0:T(8,128)(2,1)} %copy-done.11, bf16[128,1024]{1,0:T(8,128)(2,1)} %copy-done.12, ...), custom_call_target="tpu_custom_call", output_to_operand_aliasing={{}: (13, {})} | custom-call | flops 3450000896 | bytes 1024 | tf_op jit(solution)/shard_map/pallas_call | solution.py:466
  (98 shorter events, 10.9 us)
Async XLA Ops:
  1.6 23.4 %collective-permute-start = (bf16[4,2,64,256]{3,2,1,0:T(8,128)(2,1)S(1)}, bf16[4,2,64,256]{3,2,1,0:T(8,128)(2,1)S(1)}, u32[]{:S(2)}, u32[]{:S(2)}) collective-permute-start(bf16[4,2,64,256]{3,2,1,0:T(8,128)(2,1)S(1)} %bitcast.48), channel_id=1, source_target_pairs={{0,16},{4,20},{8,24},{12,28},{16,0},{20,4},{24,8},{28,12},{1,17},{... | collective-permute-start | bytes 786440 | tf_op jit(solution)/shard_map/ppermute | solution.py:76
  7.0 50.4 %copy-start.2 = (bf16[1,16,64,256]{3,2,1,0:T(8,128)(2,1)}, bf16[1,16,64,256]{3,2,1,0:T(8,128)(2,1)S(1)}, u32[]{:S(2)}) copy-start(bf16[1,16,64,256]{3,2,1,0:T(8,128)(2,1)S(1)} %get-tuple-element.92) | copy-start | bytes 1572868
  7.0 92.3 %copy-start.1 = (bf16[1,16,64,256]{3,2,1,0:T(8,128)(2,1)}, bf16[1,16,64,256]{3,2,1,0:T(8,128)(2,1)S(1)}, u32[]{:S(2)}) copy-start(bf16[1,16,64,256]{3,2,1,0:T(8,128)(2,1)S(1)} %get-tuple-element.93) | copy-start | bytes 1572868
  7.0 24.3 %collective-permute-start.1 = (bf16[1024,256]{1,0:T(8,128)(2,1)S(1)}, bf16[1024,256]{1,0:T(8,128)(2,1)S(1)}, u32[]{:S(2)}, u32[]{:S(2)}) collective-permute-start(bf16[1024,256]{1,0:T(8,128)(2,1)S(1)} %bitcast.45), channel_id=1, source_target_pairs={{0,8},{4,12},{8,0},{12,4},{16,24},{20,28},{24,16},{28,20},{1,9},{5... | collective-permute-start | bytes 1572872 | tf_op jit(solution)/shard_map/ppermute | solution.py:76
  8.7 32.5 %collective-permute-start.2 = (bf16[2048,256]{1,0:T(8,128)(2,1)}, bf16[2048,256]{1,0:T(8,128)(2,1)S(1)}, u32[]{:S(2)}, u32[]{:S(2)}) collective-permute-start(bf16[2048,256]{1,0:T(8,128)(2,1)} %bitcast.21), channel_id=1, source_target_pairs={{0,4},{4,0},{8,12},{12,8},{16,20},{20,16},{24,28},{28,24},{1,5},{5... | collective-permute-start | bytes 3145736 | tf_op jit(solution)/shard_map/ppermute | solution.py:76
  15.3 5.2 %copy-start.20 = (s32[8]{0:T(128)S(1)}, s32[8]{0:T(128)}, u32[]{:S(2)}) copy-start(s32[8]{0:T(128)} %param.41) | copy-start | bytes 100
  15.3 5.9 %copy-start.21 = (s32[8]{0:T(128)S(1)}, s32[8]{0:T(128)}, u32[]{:S(2)}) copy-start(s32[8]{0:T(128)} %param.39) | copy-start | bytes 100
  15.3 7.2 %copy-start.15 = (f32[32]{0:T(128)S(1)}, f32[32]{0:T(128)}, u32[]{:S(2)}) copy-start(f32[32]{0:T(128)} %param.33) | copy-start | bytes 388
  15.3 7.3 %copy-start.16 = (f32[32]{0:T(128)S(1)}, f32[32]{0:T(128)}, u32[]{:S(2)}) copy-start(f32[32]{0:T(128)} %param.34) | copy-start | bytes 388
  15.4 8.5 %copy-start.17 = (f32[32]{0:T(128)S(1)}, f32[32]{0:T(128)}, u32[]{:S(2)}) copy-start(f32[32]{0:T(128)} %param.35) | copy-start | bytes 388
  15.4 63.5 %all-to-all-start = ((bf16[4,128,4864]{2,1,0:T(8,128)(2,1)}), bf16[4,128,4864]{2,1,0:T(8,128)(2,1)}, u32[]{:S(2)}, u32[]{:S(2)}) async-start(bf16[4,128,4864]{2,1,0:T(8,128)(2,1)} %shard_map.176), calls=%async_computation | async-start | bytes 9961472 | tf_op jit(solution)/shard_map/all_to_all | solution.py:71
  26.0 33.4 %collective-permute-start.5 = (bf16[8,2,64,256]{3,2,1,0:T(8,128)(2,1)}, bf16[8,2,64,256]{3,2,1,0:T(8,128)(2,1)}, u32[]{:S(2)}, u32[]{:S(2)}) collective-permute-start(bf16[8,2,64,256]{3,2,1,0:T(8,128)(2,1)} %shard_map.177.refs_0_), channel_id=1, source_target_pairs={{0,4},{4,0},{8,12},{12,8},{16,20},{20,16},{24,28},{28,24},{1,5},{5... | collective-permute-start | bytes 1572872 | tf_op jit(solution)/shard_map/ppermute | solution.py:76
  26.5 14.3 %collective-permute-start.4 = (bf16[8,2,64,256]{3,2,1,0:T(8,128)(2,1)}, bf16[8,2,64,256]{3,2,1,0:T(8,128)(2,1)}, u32[]{:S(2)}, u32[]{:S(2)}) collective-permute-start(bf16[8,2,64,256]{3,2,1,0:T(8,128)(2,1)} %shard_map.177.refs_0_), channel_id=1, source_target_pairs={{0,8},{4,12},{8,0},{12,4},{16,24},{20,28},{24,16},{28,20},{1,9},{5... | collective-permute-start | bytes 1572872 | tf_op jit(solution)/shard_map/ppermute | solution.py:76
  28.7 50.2 %copy-start.22 = (s32[32]{0:T(128)}, s32[32]{0:T(128)S(1)}, u32[]{:S(2)}) copy-start(s32[32]{0:T(128)S(1)} %convert_reduce_fusion.1.often_ref) | copy-start | bytes 388
  31.3 63.8 %copy-start.3 = (bf16[1024,256]{1,0:T(8,128)(2,1)}, bf16[1024,256]{1,0:T(8,128)(2,1)S(1)}, u32[]{:S(2)}) copy-start(bf16[1024,256]{1,0:T(8,128)(2,1)S(1)} %collective-permute-done.1.refs_1_) | copy-start | bytes 1572868
  31.3 26.2 %collective-permute-start.3 = (bf16[1024,256]{1,0:T(8,128)(2,1)S(1)}, bf16[1024,256]{1,0:T(8,128)(2,1)S(1)}, u32[]{:S(2)}, u32[]{:S(2)}) collective-permute-start(bf16[1024,256]{1,0:T(8,128)(2,1)S(1)} %collective-permute-done.1.refs_1_), channel_id=1, source_target_pairs={{0,4},{4,0},{8,12},{12,8},{16,20},{20,16},{24,28},{28,24},{1,5},{5... | collective-permute-start | bytes 1572872 | tf_op jit(solution)/shard_map/ppermute | solution.py:76
  40.8 36.5 %collective-permute-start.7 = (bf16[1024,256]{1,0:T(8,128)(2,1)S(1)}, bf16[1024,256]{1,0:T(8,128)(2,1)S(1)}, u32[]{:S(2)}, u32[]{:S(2)}) collective-permute-start(bf16[1024,256]{1,0:T(8,128)(2,1)S(1)} %bitcast.42), channel_id=1, source_target_pairs={{0,16},{4,20},{8,24},{12,28},{16,0},{20,4},{24,8},{28,12},{1,17},{... | collective-permute-start | bytes 1572872 | tf_op jit(solution)/shard_map/ppermute | solution.py:76
  41.2 58.2 %copy-start = (bf16[2048,256]{1,0:T(8,128)(2,1)}, bf16[2048,256]{1,0:T(8,128)(2,1)S(1)}, u32[]{:S(2)}) copy-start(bf16[2048,256]{1,0:T(8,128)(2,1)S(1)} %collective-permute-done.2.refs_2_) | copy-start | bytes 3145732
  41.2 37.7 %collective-permute-start.6 = (bf16[8,2,64,256]{3,2,1,0:T(8,128)(2,1)}, bf16[8,2,64,256]{3,2,1,0:T(8,128)(2,1)}, u32[]{:S(2)}, u32[]{:S(2)}) collective-permute-start(bf16[8,2,64,256]{3,2,1,0:T(8,128)(2,1)} %collective-permute-done.4.refs_1_), channel_id=1, source_target_pairs={{0,4},{4,0},{8,12},{12,8},{16,20},{20,16},{24,28},{28,24},{1,5},{5... | collective-permute-start | bytes 1572872 | tf_op jit(solution)/shard_map/ppermute | solution.py:76
  57.5 19.9 %copy-start.5 = (bf16[1024,256]{1,0:T(8,128)(2,1)}, bf16[1024,256]{1,0:T(8,128)(2,1)S(1)}, u32[]{:S(2)}) copy-start(bf16[1024,256]{1,0:T(8,128)(2,1)S(1)} %collective-permute-done.3.refs_3_) | copy-start | bytes 1572868
  59.0 41.4 %collective-permute-start.13 = (bf16[1024,256]{1,0:T(8,128)(2,1)}, bf16[1024,256]{1,0:T(8,128)(2,1)}, u32[]{:S(2)}, u32[]{:S(2)}) collective-permute-start(bf16[1024,256]{1,0:T(8,128)(2,1)} %shard_map.178), channel_id=1, source_target_pairs={{0,16},{4,20},{8,24},{12,28},{16,0},{20,4},{24,8},{28,12},{1,17},{... | collective-permute-start | bytes 1572872 | tf_op jit(solution)/shard_map/ppermute | solution.py:76
  77.3 22.0 %copy-start.4 = (bf16[1024,256]{1,0:T(8,128)(2,1)}, bf16[1024,256]{1,0:T(8,128)(2,1)S(1)}, u32[]{:S(2)}) copy-start(bf16[1024,256]{1,0:T(8,128)(2,1)S(1)} %collective-permute-done.7.refs_1_) | copy-start | bytes 1572868
  77.3 22.0 %collective-permute-start.8 = (bf16[1024,256]{1,0:T(8,128)(2,1)S(1)}, bf16[1024,256]{1,0:T(8,128)(2,1)S(1)}, u32[]{:S(2)}, u32[]{:S(2)}) collective-permute-start(bf16[1024,256]{1,0:T(8,128)(2,1)S(1)} %collective-permute-done.7.refs_1_), channel_id=1, source_target_pairs={{0,4},{4,0},{8,12},{12,8},{16,20},{20,16},{24,28},{28,24},{1,5},{5... | collective-permute-start | bytes 1572872 | tf_op jit(solution)/shard_map/ppermute | solution.py:76
  95.1 35.9 %all-to-all-start.1 = ((bf16[4,128,1024]{2,1,0:T(8,128)(2,1)}), bf16[4,128,1024]{2,1,0:T(8,128)(2,1)}, u32[]{:S(2)}, u32[]{:S(2)}) async-start(bf16[4,128,1024]{2,1,0:T(8,128)(2,1)} %shard_map.179), calls=%async_computation.1 | async-start | bytes 2097152 | tf_op jit(solution)/shard_map/all_to_all | solution.py:71
  99.4 9.9 %copy-start.6 = (bf16[1024,256]{1,0:T(8,128)(2,1)}, bf16[1024,256]{1,0:T(8,128)(2,1)S(1)}, u32[]{:S(2)}) copy-start(bf16[1024,256]{1,0:T(8,128)(2,1)S(1)} %collective-permute-done.8.refs_3_) | copy-start | bytes 1572868
  100.3 14.3 %collective-permute-start.9 = (bf16[1024,256]{1,0:T(8,128)(2,1)S(1)}, bf16[1024,256]{1,0:T(8,128)(2,1)S(1)}, u32[]{:S(2)}, u32[]{:S(2)}) collective-permute-start(bf16[1024,256]{1,0:T(8,128)(2,1)S(1)} %shard_map.180), channel_id=1, source_target_pairs={{0,8},{4,12},{8,0},{12,4},{16,24},{20,28},{24,16},{28,20},{1,9},{5... | collective-permute-start | bytes 1572872 | tf_op jit(solution)/shard_map/ppermute | solution.py:76
  109.3 16.9 %collective-permute-start.14 = (bf16[128,1024]{1,0:T(8,128)(2,1)}, bf16[128,1024]{1,0:T(8,128)(2,1)S(1)}, u32[]{:S(2)}, u32[]{:S(2)}) collective-permute-start(bf16[128,1024]{1,0:T(8,128)(2,1)} %get-tuple-element.89), channel_id=1, source_target_pairs={{0,1},{1,0},{2,3},{3,2},{4,5},{5,4},{6,7},{7,6},{8,9},{9,8},{10,11... | collective-permute-start | bytes 786440 | tf_op jit(solution)/shard_map/ppermute | solution.py:76
  109.8 16.5 %collective-permute-start.15 = (bf16[128,1024]{1,0:T(8,128)(2,1)}, bf16[128,1024]{1,0:T(8,128)(2,1)S(1)}, u32[]{:S(2)}, u32[]{:S(2)}) collective-permute-start(bf16[128,1024]{1,0:T(8,128)(2,1)} %get-tuple-element.90), channel_id=1, source_target_pairs={{0,2},{1,3},{2,0},{3,1},{4,6},{5,7},{6,4},{7,5},{8,10},{9,11},{10,... | collective-permute-start | bytes 786440 | tf_op jit(solution)/shard_map/ppermute | solution.py:76
  111.5 14.8 %collective-permute-start.16 = (bf16[128,1024]{1,0:T(8,128)(2,1)}, bf16[128,1024]{1,0:T(8,128)(2,1)S(1)}, u32[]{:S(2)}, u32[]{:S(2)}) collective-permute-start(bf16[128,1024]{1,0:T(8,128)(2,1)} %get-tuple-element.91), channel_id=1, source_target_pairs={{0,3},{1,2},{2,1},{3,0},{4,7},{5,6},{6,5},{7,4},{8,11},{9,10},{10,... | collective-permute-start | bytes 786440 | tf_op jit(solution)/shard_map/ppermute | solution.py:76
  124.3 9.4 %collective-permute-start.10 = (bf16[128,1024]{1,0:T(8,128)(2,1)}, bf16[128,1024]{1,0:T(8,128)(2,1)S(1)}, u32[]{:S(2)}, u32[]{:S(2)}) collective-permute-start(bf16[128,1024]{1,0:T(8,128)(2,1)} %get-tuple-element.84), channel_id=1, source_target_pairs={{0,1},{1,0},{2,3},{3,2},{4,5},{5,4},{6,7},{7,6},{8,9},{9,8},{10,11... | collective-permute-start | bytes 786440 | tf_op jit(solution)/shard_map/ppermute | solution.py:76
  124.4 9.4 %collective-permute-start.11 = (bf16[128,1024]{1,0:T(8,128)(2,1)}, bf16[128,1024]{1,0:T(8,128)(2,1)S(1)}, u32[]{:S(2)}, u32[]{:S(2)}) collective-permute-start(bf16[128,1024]{1,0:T(8,128)(2,1)} %get-tuple-element.85), channel_id=1, source_target_pairs={{0,2},{1,3},{2,0},{3,1},{4,6},{5,7},{6,4},{7,5},{8,10},{9,11},{10,... | collective-permute-start | bytes 786440 | tf_op jit(solution)/shard_map/ppermute | solution.py:76
  126.1 12.4 %collective-permute-start.12 = (bf16[128,1024]{1,0:T(8,128)(2,1)}, bf16[128,1024]{1,0:T(8,128)(2,1)S(1)}, u32[]{:S(2)}, u32[]{:S(2)}) collective-permute-start(bf16[128,1024]{1,0:T(8,128)(2,1)} %get-tuple-element.86), channel_id=1, source_target_pairs={{0,3},{1,2},{2,1},{3,0},{4,7},{5,6},{6,5},{7,4},{8,11},{9,10},{10,... | collective-permute-start | bytes 786440 | tf_op jit(solution)/shard_map/ppermute | solution.py:76
  (10 other events, 17.1 us)

commit v3 on v2

--- a/solution.py
+++ b/solution.py
@@ -557,7 +557,7 @@
     pool_own = jnp.transpose(block_pool, (0, 2, 1, 3))
     state_own = state_pool.reshape(local_groups * group_width, STATE)
     state_groups = [state_own[group * group_width : (group + 1) * group_width] for group in range(local_groups)]
-    packed = pack(parts, pieces, after(norm_gain, pool_own, *state_groups).reshape(-1, 128))
+    packed = pack(parts, pieces, after(norm_gain, pool_own).reshape(-1, 128))
     joined = spread(packed)
 
     far_mask = 1 << order[1]
@@ -577,7 +577,7 @@
     state_lists, begun = [None] * local_groups, []
 
     def fetch(group, last_gate):
-        gates = ([pools[1][0]], [pools[2][0]]) if group % 2 == 0 else ([], [])
+        gates = ([pool_far], [array for array, _ in pools[1:3]]) if group % 2 == 0 else ([], [])
         source, values, sent = fetch_state(
             state_groups[group], state_far, far_mask, entries, bit_order(owners, group), *gates, last_gate, group
         )

time: 144 us -> 142 us (0.986)
  waiting for transfers between devices: 45.4 us -> 43.4 us
    ppermute x17, waiting for transfers between devices: 45.4 us -> 35 us  [swap(): return lax.ppermute(value, axis, [(i, i ^ mask) for i in range(count)])]
    all_to_all x2, waiting for transfers between devices: 0.01 us -> 8.4 us  [spread(): return lax.all_to_all(packed, 'tp', split_axis=0, concat_axis=0, tiled=True)]
  transfers between devices with their start and end apart: 19 -> 19, of which waited for: 5 -> 6; matrix products, arithmetic and copies ran while one was open for 9% -> 9% of each run, Pallas kernels for 34% -> 35%
where the time goes in v3:
time: 142 us
  Pallas kernels  52.8 us (37%)
  waiting for transfers between devices  43.4 us (31%)
  starting transfers between devices  26.6 us (19%)
  local copies, waits for them, and re-layouts  9.57 us (7%)
  other arithmetic  7.41 us (5%)
  between operations  1.72 us (1%)
    ppermute x17, waiting for transfers between devices, swap(): return lax.ppermute(value, axis, [(i, i ^ mask) for i in range(count)])  35 us
    pallas_call x2, Pallas kernels, scan_group(): pl.pallas_call(functools.partial(scan_body, parts, sources, heads, group)...  17.7 us
    ppermute x17, starting transfers between devices, swap(): return lax.ppermute(value, axis, [(i, i ^ mask) for i in range(count)])  17.2 us
    pallas_call x1, Pallas kernels, attention(): pl.pallas_call(functools.partial(attention_body, parts, [offsets for _, o...  16.2 us
    all_to_all x2, starting transfers between devices, spread(): return lax.all_to_all(packed, 'tp', split_axis=0, concat_axis=0, tiled=True)  9.41 us
    all_to_all x2, waiting for transfers between devices, spread(): return lax.all_to_all(packed, 'tp', split_axis=0, concat_axis=0, tiled=True)  8.4 us
    pallas_call x2, Pallas kernels, norm_group(): pl.pallas_call(functools.partial(norm_body, parts, group, local_groups),...  7.8 us
    pallas_call x1, Pallas kernels, pack(): pl.pallas_call(body, grid=(parts,), in_specs=specs + [pl.BlockSpec(gain.s...  5.12 us
  transfers between devices with their start and end apart: 19, of which 6 were waited for; matrix products, arithmetic and copies ran while one was open for 9% of the time, Pallas kernels for 35%

profile of v3, /device:TPU:0, one launch (start us, length us, event | category | flops | bytes accessed | tf_op | source)
XLA Modules:
  0.0 141.5 jit_solution(16485328952588969663)
XLA Ops:
  0.6 1.0 copy.23
  1.6 4.1 %collective-permute-start = (bf16[4,2,64,256]{3,2,1,0:T(8,128)(2,1)S(1)}, bf16[4,2,64,256]{3,2,1,0:T(8,128)(2,1)S(1)}, u32[]{:S(2)}, u32[]{:S(2)}) collective-permute-start(bf16[4,2,64,256]{3,2,1,0:T(8,128)(2,1)S(1)} %bitcast.48), channel_id=1, source_target_pairs={{0,16},{4,20},{8,24},{12,28},{16,0},{20,4},{24,8},{28,12},{1,17},{... | collective-permute-start | bytes 786440 | tf_op jit(solution)/shard_map/ppermute | solution.py:76
  5.7 1.3 fusion.15
  7.0 1.6 %collective-permute-start.1 = (bf16[1024,256]{1,0:T(8,128)(2,1)S(1)}, bf16[1024,256]{1,0:T(8,128)(2,1)S(1)}, u32[]{:S(2)}, u32[]{:S(2)}) collective-permute-start(bf16[1024,256]{1,0:T(8,128)(2,1)S(1)} %bitcast.45), channel_id=1, source_target_pairs={{0,8},{4,12},{8,0},{12,4},{16,24},{20,28},{24,16},{28,20},{1,9},{5... | collective-permute-start | bytes 1572872 | tf_op jit(solution)/shard_map/ppermute | solution.py:76
  8.7 1.5 %collective-permute-start.2 = (bf16[2048,256]{1,0:T(8,128)(2,1)}, bf16[2048,256]{1,0:T(8,128)(2,1)S(1)}, u32[]{:S(2)}, u32[]{:S(2)}) collective-permute-start(bf16[2048,256]{1,0:T(8,128)(2,1)} %bitcast.20), channel_id=1, source_target_pairs={{0,4},{4,0},{8,12},{12,8},{16,20},{20,16},{24,28},{28,24},{1,5},{5... | collective-permute-start | bytes 3145736 | tf_op jit(solution)/shard_map/ppermute | solution.py:76
  10.2 5.1 %shard_map.176 = bf16[4,128,4864]{2,1,0:T(8,128)(2,1)} custom-call(bf16[128,8192]{1,0:T(8,128)(2,1)} %bitcast.59, bf16[128,4096]{1,0:T(8,128)(2,1)} %bitcast.60, bf16[128,4096]{1,0:T(8,128)(2,1)} %bitcast.61, bf16[128,2048]{1,0:T(8,128)(2,1)} %bitcast.62, bf16[128,128]{1,0:T(8,128)(2,1)} %bitcast.63, f32[16,128]{1,0:T(8,128)} %bitcast.64), custom_call_target="tpu_custom_call" | custom-call | flops 1024 | bytes 1024 | tf_op jit(solution)/shard_map/pallas_call | solution.py:59
  15.4 5.2 %all-to-all-start = ((bf16[4,128,4864]{2,1,0:T(8,128)(2,1)}), bf16[4,128,4864]{2,1,0:T(8,128)(2,1)}, u32[]{:S(2)}, u32[]{:S(2)}) async-start(bf16[4,128,4864]{2,1,0:T(8,128)(2,1)} %shard_map.176), calls=%async_computation | async-start | bytes 9961472 | tf_op jit(solution)/shard_map/all_to_all | solution.py:71
  25.0 0.9 shard_map.177.refs_0_
  29.4 1.3 pad_add_fusion.4.where_ref
  31.4 1.8 %collective-permute-start.3 = (bf16[1024,256]{1,0:T(8,128)(2,1)S(1)}, bf16[1024,256]{1,0:T(8,128)(2,1)S(1)}, u32[]{:S(2)}, u32[]{:S(2)}) collective-permute-start(bf16[1024,256]{1,0:T(8,128)(2,1)S(1)} %collective-permute-done.1.refs_1_), channel_id=1, source_target_pairs={{0,4},{4,0},{8,12},{12,8},{16,20},{20,16},{24,28},{28,24},{1,5},{5... | collective-permute-start | bytes 1572872 | tf_op jit(solution)/shard_map/ppermute | solution.py:76
  33.3 16.9 %collective-permute-done.4.refs_1_ = bf16[8,2,64,256]{3,2,1,0:T(8,128)(2,1)} collective-permute-done((bf16[8,2,64,256]{3,2,1,0:T(8,128)(2,1)}, bf16[8,2,64,256]{3,2,1,0:T(8,128)(2,1)}, u32[]{:S(2)}, u32[]{:S(2)}) %collective-permute-start.4) | collective-permute-done | bytes 524320 | tf_op jit(solution)/shard_map/ppermute | solution.py:76
  50.2 1.5 %collective-permute-start.6 = (bf16[8,2,64,256]{3,2,1,0:T(8,128)(2,1)}, bf16[8,2,64,256]{3,2,1,0:T(8,128)(2,1)}, u32[]{:S(2)}, u32[]{:S(2)}) collective-permute-start(bf16[8,2,64,256]{3,2,1,0:T(8,128)(2,1)} %collective-permute-done.4.refs_1_), channel_id=1, source_target_pairs={{0,4},{4,0},{8,12},{12,8},{16,20},{20,16},{24,28},{28,24},{1,5},{5... | collective-permute-start | bytes 1572872 | tf_op jit(solution)/shard_map/ppermute | solution.py:76
  51.7 1.3 pad_add_fusion.3.where_ref
  53.1 1.3 pad_add_fusion.5.where_ref
  55.6 1.9 %collective-permute-done.3.refs_3_ = bf16[1024,256]{1,0:T(8,128)(2,1)S(1)} collective-permute-done((bf16[1024,256]{1,0:T(8,128)(2,1)S(1)}, bf16[1024,256]{1,0:T(8,128)(2,1)S(1)}, u32[]{:S(2)}, u32[]{:S(2)}) %collective-permute-start.3) | collective-permute-done | bytes 524320 | tf_op jit(solution)/shard_map/ppermute | solution.py:76
  57.5 1.5 %shard_map.178 = bf16[1024,256]{1,0:T(8,128)(2,1)} custom-call(s32[1]{0:T(128)} %bitcast.18.index_ref, bf16[1024,256]{1,0:T(8,128)(2,1)S(1)} %bitcast.46, bf16[1024,256]{1,0:T(8,128)(2,1)S(1)} %collective-permute-done.1.refs_1_, bf16[2048,256]{1,0:T(8,128)(2,1)S(1)} %collective-permute-done.2.refs_2_, bf16[1024,256]{1,0:T(8,128)(2,1)S(1)} %collective-permute-done.3.refs_3_), custom_call_target="tpu_custom_call" | custom-call | flops 1024 | bytes 1024 | tf_op jit(solution)/shard_map/pallas_call | solution.py:353
  59.4 9.4 %collective-permute-done.6.refs_3_ = bf16[8,2,64,256]{3,2,1,0:T(8,128)(2,1)} collective-permute-done((bf16[8,2,64,256]{3,2,1,0:T(8,128)(2,1)}, bf16[8,2,64,256]{3,2,1,0:T(8,128)(2,1)}, u32[]{:S(2)}, u32[]{:S(2)}) %collective-permute-start.6) | collective-permute-done | bytes 524320 | tf_op jit(solution)/shard_map/ppermute | solution.py:76
  68.8 8.4 %all-to-all-done.q_ref.refs_8_.refs_9_.refs_10_.refs_11_ = bf16[4,128,4864]{2,1,0:T(8,128)(2,1)} async-done(((bf16[4,128,4864]{2,1,0:T(8,128)(2,1)}), bf16[4,128,4864]{2,1,0:T(8,128)(2,1)}, u32[]{:S(2)}, u32[]{:S(2)}) %all-to-all-start) | async-done | bytes 4980768 | tf_op jit(solution)/shard_map/all_to_all | solution.py:71
  77.2 16.2 %shard_map.179 = bf16[4,128,1024]{2,1,0:T(8,128)(2,1)} custom-call(s32[2]{0:T(128)} %pad_add_fusion.4.where_ref, s32[32]{0:T(128)} %copy-done.22, s32[32]{0:T(128)} %convert_reduce_fusion.place_ref, bf16[4,128,4864]{2,1,0:T(8,128)(2,1)} %all-to-all-done.q_ref.refs_8_.refs_9_.refs_10_.refs_11_, bf16[512,4864]{1,0:T(8,128)(2,1)} %bitcast.21.fresh_ref.x_ref.proj_ref.raw_ref, ...), custom_call_target="tpu_custom_call" | custom-call | flops 18400002048 | bytes 1024 | tf_op jit(solution)/shard_map/pallas_call | solution.py:193
  93.4 4.3 %all-to-all-start.1 = ((bf16[4,128,1024]{2,1,0:T(8,128)(2,1)}), bf16[4,128,1024]{2,1,0:T(8,128)(2,1)}, u32[]{:S(2)}, u32[]{:S(2)}) async-start(bf16[4,128,1024]{2,1,0:T(8,128)(2,1)} %shard_map.179), calls=%async_computation.1 | async-start | bytes 2097152 | tf_op jit(solution)/shard_map/all_to_all | solution.py:71
  97.7 0.9 shard_map.180
  99.1 0.8 copy-done.18
  99.9 8.8 %shard_map.183 = (bf16[128,1024]{1,0:T(8,128)(2,1)}, bf16[128,1024]{1,0:T(8,128)(2,1)}, bf16[128,1024]{1,0:T(8,128)(2,1)}, bf16[128,1024]{1,0:T(8,128)(2,1)}) custom-call(s32[3]{0:T(128)} %pad_add_fusion.5.where_ref, bf16[512,4864]{1,0:T(8,128)(2,1)} %bitcast.21.fresh_ref.x_ref.proj_ref.raw_ref, bf16[512,4864]{1,0:T(8,128)(2,1)} %bitcast.21.fresh_ref.x_ref.proj_ref.raw_ref, ...), custom_call_target="tpu_custom_call" | custom-call | flops 9200001024 | bytes 1024 | tf_op jit(solution)/shard_map/pallas_call | solution.py:316
  109.0 1.9 %collective-permute-start.15 = (bf16[128,1024]{1,0:T(8,128)(2,1)}, bf16[128,1024]{1,0:T(8,128)(2,1)S(1)}, u32[]{:S(2)}, u32[]{:S(2)}) collective-permute-start(bf16[128,1024]{1,0:T(8,128)(2,1)} %get-tuple-element.90), channel_id=1, source_target_pairs={{0,2},{1,3},{2,0},{3,1},{4,6},{5,7},{6,4},{7,5},{8,10},{9,11},{10,... | collective-permute-start | bytes 786440 | tf_op jit(solution)/shard_map/ppermute | solution.py:76
  110.9 2.0 %collective-permute-done.9.refs_4_ = bf16[1024,256]{1,0:T(8,128)(2,1)S(1)} collective-permute-done((bf16[1024,256]{1,0:T(8,128)(2,1)S(1)}, bf16[1024,256]{1,0:T(8,128)(2,1)S(1)}, u32[]{:S(2)}, u32[]{:S(2)}) %collective-permute-start.9) | collective-permute-done | bytes 524320 | tf_op jit(solution)/shard_map/ppermute | solution.py:76
  112.9 0.8 copy-done.19
  113.7 8.8 %shard_map.181 = (bf16[128,1024]{1,0:T(8,128)(2,1)}, bf16[128,1024]{1,0:T(8,128)(2,1)}, bf16[128,1024]{1,0:T(8,128)(2,1)}, bf16[128,1024]{1,0:T(8,128)(2,1)}) custom-call(s32[3]{0:T(128)} %pad_add_fusion.3.where_ref, bf16[512,4864]{1,0:T(8,128)(2,1)} %bitcast.21.fresh_ref.x_ref.proj_ref.raw_ref, bf16[512,4864]{1,0:T(8,128)(2,1)} %bitcast.21.fresh_ref.x_ref.proj_ref.raw_ref, ...), custom_call_target="tpu_custom_call" | custom-call | flops 9200001024 | bytes 1024 | tf_op jit(solution)/shard_map/pallas_call | solution.py:316
  122.7 1.7 %collective-permute-start.11 = (bf16[128,1024]{1,0:T(8,128)(2,1)}, bf16[128,1024]{1,0:T(8,128)(2,1)S(1)}, u32[]{:S(2)}, u32[]{:S(2)}) collective-permute-start(bf16[128,1024]{1,0:T(8,128)(2,1)} %get-tuple-element.85), channel_id=1, source_target_pairs={{0,2},{1,3},{2,0},{3,1},{4,6},{5,7},{6,4},{7,5},{8,10},{9,11},{10,... | collective-permute-start | bytes 786440 | tf_op jit(solution)/shard_map/ppermute | solution.py:76
  125.3 3.9 %shard_map.184.refs_12_ = bf16[128,8192]{1,0:T(8,128)(2,1)} custom-call(s32[2]{0:T(128)} %pad_add_fusion.2.where_ref, bf16[128,1024]{1,0:T(8,128)(2,1)} %get-tuple-element.88.refs_0_, bf16[128,1024]{1,0:T(8,128)(2,1)} %copy-done.6, bf16[128,1024]{1,0:T(8,128)(2,1)} %copy-done.7, bf16[128,1024]{1,0:T(8,128)(2,1)} %copy-done.9, bf16[128,8192]{1,0:T(8,128)(2,1)} %bitcast.50, ...), custom_call_target="tpu_custom_call" | custom-call | flops 3450000896 | bytes 1024 | tf_op jit(solution)/shard_map/pallas_call | solution.py:466
  129.2 2.8 %shard_map.182 = bf16[128,4096]{1,0:T(8,128)(2,1)} custom-call(s32[2]{0:T(128)} %pad_add_fusion.2.where_ref, bf16[4,128,1024]{2,1,0:T(8,128)(2,1)} %all-to-all-done.1.in_ref), custom_call_target="tpu_custom_call" | custom-call | flops 2300001024 | bytes 1024 | tf_op jit(solution)/shard_map/pallas_call | solution.py:496
  132.1 4.7 %collective-permute-done.12.refs_3_ = bf16[128,1024]{1,0:T(8,128)(2,1)S(1)} collective-permute-done((bf16[128,1024]{1,0:T(8,128)(2,1)}, bf16[128,1024]{1,0:T(8,128)(2,1)S(1)}, u32[]{:S(2)}, u32[]{:S(2)}) %collective-permute-start.12) | collective-permute-done | bytes 262176 | tf_op jit(solution)/shard_map/ppermute | solution.py:76
  137.5 3.9 %shard_map.185 = bf16[128,8192]{1,0:T(8,128)(2,1)} custom-call(s32[2]{0:T(128)} %pad_add_fusion.2.where_ref, bf16[128,1024]{1,0:T(8,128)(2,1)} %get-tuple-element.81.refs_0_, bf16[128,1024]{1,0:T(8,128)(2,1)} %copy-done.8, bf16[128,1024]{1,0:T(8,128)(2,1)} %copy-done.10, bf16[128,1024]{1,0:T(8,128)(2,1)} %copy-done.11, ...), custom_call_target="tpu_custom_call", output_to_operand_aliasing={{}: (13, {})} | custom-call | flops 3450000896 | bytes 1024 | tf_op jit(solution)/shard_map/pallas_call | solution.py:466
  (98 shorter events, 12.1 us)
Async XLA Ops:
  1.6 23.4 %collective-permute-start = (bf16[4,2,64,256]{3,2,1,0:T(8,128)(2,1)S(1)}, bf16[4,2,64,256]{3,2,1,0:T(8,128)(2,1)S(1)}, u32[]{:S(2)}, u32[]{:S(2)}) collective-permute-start(bf16[4,2,64,256]{3,2,1,0:T(8,128)(2,1)S(1)} %bitcast.48), channel_id=1, source_target_pairs={{0,16},{4,20},{8,24},{12,28},{16,0},{20,4},{24,8},{28,12},{1,17},{... | collective-permute-start | bytes 786440 | tf_op jit(solution)/shard_map/ppermute | solution.py:76
  7.0 50.4 %copy-start.2 = (bf16[1,16,64,256]{3,2,1,0:T(8,128)(2,1)}, bf16[1,16,64,256]{3,2,1,0:T(8,128)(2,1)S(1)}, u32[]{:S(2)}) copy-start(bf16[1,16,64,256]{3,2,1,0:T(8,128)(2,1)S(1)} %get-tuple-element.93) | copy-start | bytes 1572868
  7.0 90.7 %copy-start.1 = (bf16[1,16,64,256]{3,2,1,0:T(8,128)(2,1)}, bf16[1,16,64,256]{3,2,1,0:T(8,128)(2,1)S(1)}, u32[]{:S(2)}) copy-start(bf16[1,16,64,256]{3,2,1,0:T(8,128)(2,1)S(1)} %get-tuple-element.92) | copy-start | bytes 1572868
  7.0 24.4 %collective-permute-start.1 = (bf16[1024,256]{1,0:T(8,128)(2,1)S(1)}, bf16[1024,256]{1,0:T(8,128)(2,1)S(1)}, u32[]{:S(2)}, u32[]{:S(2)}) collective-permute-start(bf16[1024,256]{1,0:T(8,128)(2,1)S(1)} %bitcast.45), channel_id=1, source_target_pairs={{0,8},{4,12},{8,0},{12,4},{16,24},{20,28},{24,16},{28,20},{1,9},{5... | collective-permute-start | bytes 1572872 | tf_op jit(solution)/shard_map/ppermute | solution.py:76
  8.7 41.5 %collective-permute-start.2 = (bf16[2048,256]{1,0:T(8,128)(2,1)}, bf16[2048,256]{1,0:T(8,128)(2,1)S(1)}, u32[]{:S(2)}, u32[]{:S(2)}) collective-permute-start(bf16[2048,256]{1,0:T(8,128)(2,1)} %bitcast.20), channel_id=1, source_target_pairs={{0,4},{4,0},{8,12},{12,8},{16,20},{20,16},{24,28},{28,24},{1,5},{5... | collective-permute-start | bytes 3145736 | tf_op jit(solution)/shard_map/ppermute | solution.py:76
  15.3 5.2 %copy-start.20 = (s32[8]{0:T(128)S(1)}, s32[8]{0:T(128)}, u32[]{:S(2)}) copy-start(s32[8]{0:T(128)} %param.41) | copy-start | bytes 100
  15.3 5.9 %copy-start.21 = (s32[8]{0:T(128)S(1)}, s32[8]{0:T(128)}, u32[]{:S(2)}) copy-start(s32[8]{0:T(128)} %param.39) | copy-start | bytes 100
  15.3 7.2 %copy-start.14 = (f32[32]{0:T(128)S(1)}, f32[32]{0:T(128)}, u32[]{:S(2)}) copy-start(f32[32]{0:T(128)} %param.33) | copy-start | bytes 388
  15.3 7.3 %copy-start.15 = (f32[32]{0:T(128)S(1)}, f32[32]{0:T(128)}, u32[]{:S(2)}) copy-start(f32[32]{0:T(128)} %param.34) | copy-start | bytes 388
  15.4 8.5 %copy-start.16 = (f32[32]{0:T(128)S(1)}, f32[32]{0:T(128)}, u32[]{:S(2)}) copy-start(f32[32]{0:T(128)} %param.35) | copy-start | bytes 388
  15.4 61.8 %all-to-all-start = ((bf16[4,128,4864]{2,1,0:T(8,128)(2,1)}), bf16[4,128,4864]{2,1,0:T(8,128)(2,1)}, u32[]{:S(2)}, u32[]{:S(2)}) async-start(bf16[4,128,4864]{2,1,0:T(8,128)(2,1)} %shard_map.176), calls=%async_computation | async-start | bytes 9961472 | tf_op jit(solution)/shard_map/all_to_all | solution.py:71
  26.0 29.0 %collective-permute-start.5 = (bf16[8,2,64,256]{3,2,1,0:T(8,128)(2,1)}, bf16[8,2,64,256]{3,2,1,0:T(8,128)(2,1)}, u32[]{:S(2)}, u32[]{:S(2)}) collective-permute-start(bf16[8,2,64,256]{3,2,1,0:T(8,128)(2,1)} %shard_map.177.refs_0_), channel_id=1, source_target_pairs={{0,4},{4,0},{8,12},{12,8},{16,20},{20,16},{24,28},{28,24},{1,5},{5... | collective-permute-start | bytes 1572872 | tf_op jit(solution)/shard_map/ppermute | solution.py:76
  26.5 23.6 %collective-permute-start.4 = (bf16[8,2,64,256]{3,2,1,0:T(8,128)(2,1)}, bf16[8,2,64,256]{3,2,1,0:T(8,128)(2,1)}, u32[]{:S(2)}, u32[]{:S(2)}) collective-permute-start(bf16[8,2,64,256]{3,2,1,0:T(8,128)(2,1)} %shard_map.177.refs_0_), channel_id=1, source_target_pairs={{0,8},{4,12},{8,0},{12,4},{16,24},{20,28},{24,16},{28,20},{1,9},{5... | collective-permute-start | bytes 1572872 | tf_op jit(solution)/shard_map/ppermute | solution.py:76
  27.9 27.2 %collective-permute-start.7 = (bf16[1024,256]{1,0:T(8,128)(2,1)S(1)}, bf16[1024,256]{1,0:T(8,128)(2,1)S(1)}, u32[]{:S(2)}, u32[]{:S(2)}) collective-permute-start(bf16[1024,256]{1,0:T(8,128)(2,1)S(1)} %bitcast.42), channel_id=1, source_target_pairs={{0,16},{4,20},{8,24},{12,28},{16,0},{20,4},{24,8},{28,12},{1,17},{... | collective-permute-start | bytes 1572872 | tf_op jit(solution)/shard_map/ppermute | solution.py:76
  28.7 48.5 %copy-start.22 = (s32[32]{0:T(128)}, s32[32]{0:T(128)S(1)}, u32[]{:S(2)}) copy-start(s32[32]{0:T(128)S(1)} %convert_reduce_fusion.1.often_ref) | copy-start | bytes 388
  31.4 62.0 %copy-start.3 = (bf16[1024,256]{1,0:T(8,128)(2,1)}, bf16[1024,256]{1,0:T(8,128)(2,1)S(1)}, u32[]{:S(2)}) copy-start(bf16[1024,256]{1,0:T(8,128)(2,1)S(1)} %collective-permute-done.1.refs_1_) | copy-start | bytes 1572868
  31.4 26.1 %collective-permute-start.3 = (bf16[1024,256]{1,0:T(8,128)(2,1)S(1)}, bf16[1024,256]{1,0:T(8,128)(2,1)S(1)}, u32[]{:S(2)}, u32[]{:S(2)}) collective-permute-start(bf16[1024,256]{1,0:T(8,128)(2,1)S(1)} %collective-permute-done.1.refs_1_), channel_id=1, source_target_pairs={{0,4},{4,0},{8,12},{12,8},{16,20},{20,16},{24,28},{28,24},{1,5},{5... | collective-permute-start | bytes 1572872 | tf_op jit(solution)/shard_map/ppermute | solution.py:76
  50.2 47.5 %copy-start = (bf16[2048,256]{1,0:T(8,128)(2,1)}, bf16[2048,256]{1,0:T(8,128)(2,1)S(1)}, u32[]{:S(2)}) copy-start(bf16[2048,256]{1,0:T(8,128)(2,1)S(1)} %collective-permute-done.2.refs_2_) | copy-start | bytes 3145732
  50.2 18.6 %collective-permute-start.6 = (bf16[8,2,64,256]{3,2,1,0:T(8,128)(2,1)}, bf16[8,2,64,256]{3,2,1,0:T(8,128)(2,1)}, u32[]{:S(2)}, u32[]{:S(2)}) collective-permute-start(bf16[8,2,64,256]{3,2,1,0:T(8,128)(2,1)} %collective-permute-done.4.refs_1_), channel_id=1, source_target_pairs={{0,4},{4,0},{8,12},{12,8},{16,20},{20,16},{24,28},{28,24},{1,5},{5... | collective-permute-start | bytes 1572872 | tf_op jit(solution)/shard_map/ppermute | solution.py:76
  55.0 42.7 %copy-start.4 = (bf16[1024,256]{1,0:T(8,128)(2,1)}, bf16[1024,256]{1,0:T(8,128)(2,1)S(1)}, u32[]{:S(2)}) copy-start(bf16[1024,256]{1,0:T(8,128)(2,1)S(1)} %collective-permute-done.7.refs_1_) | copy-start | bytes 1572868
  55.0 42.7 %collective-permute-start.8 = (bf16[1024,256]{1,0:T(8,128)(2,1)S(1)}, bf16[1024,256]{1,0:T(8,128)(2,1)}, u32[]{:S(2)}, u32[]{:S(2)}) collective-permute-start(bf16[1024,256]{1,0:T(8,128)(2,1)S(1)} %collective-permute-done.7.refs_1_), channel_id=1, source_target_pairs={{0,4},{4,0},{8,12},{12,8},{16,20},{20,16},{24,28},{28,24},{1,5},{5... | collective-permute-start | bytes 1572872 | tf_op jit(solution)/shard_map/ppermute | solution.py:76
  59.0 40.1 %collective-permute-start.13 = (bf16[1024,256]{1,0:T(8,128)(2,1)}, bf16[1024,256]{1,0:T(8,128)(2,1)S(1)}, u32[]{:S(2)}, u32[]{:S(2)}) collective-permute-start(bf16[1024,256]{1,0:T(8,128)(2,1)} %shard_map.178), channel_id=1, source_target_pairs={{0,16},{4,20},{8,24},{12,28},{16,0},{20,4},{24,8},{28,12},{1,17},{... | collective-permute-start | bytes 1572872 | tf_op jit(solution)/shard_map/ppermute | solution.py:76
  93.4 35.8 %all-to-all-start.1 = ((bf16[4,128,1024]{2,1,0:T(8,128)(2,1)}), bf16[4,128,1024]{2,1,0:T(8,128)(2,1)}, u32[]{:S(2)}, u32[]{:S(2)}) async-start(bf16[4,128,1024]{2,1,0:T(8,128)(2,1)} %shard_map.179), calls=%async_computation.1 | async-start | bytes 2097152 | tf_op jit(solution)/shard_map/all_to_all | solution.py:71
  98.6 14.3 %collective-permute-start.9 = (bf16[1024,256]{1,0:T(8,128)(2,1)S(1)}, bf16[1024,256]{1,0:T(8,128)(2,1)S(1)}, u32[]{:S(2)}, u32[]{:S(2)}) collective-permute-start(bf16[1024,256]{1,0:T(8,128)(2,1)S(1)} %shard_map.180), channel_id=1, source_target_pairs={{0,8},{4,12},{8,0},{12,4},{16,24},{20,28},{24,16},{28,20},{1,9},{5... | collective-permute-start | bytes 1572872 | tf_op jit(solution)/shard_map/ppermute | solution.py:76
  108.7 15.7 %collective-permute-start.14 = (bf16[128,1024]{1,0:T(8,128)(2,1)}, bf16[128,1024]{1,0:T(8,128)(2,1)S(1)}, u32[]{:S(2)}, u32[]{:S(2)}) collective-permute-start(bf16[128,1024]{1,0:T(8,128)(2,1)} %get-tuple-element.89), channel_id=1, source_target_pairs={{0,1},{1,0},{2,3},{3,2},{4,5},{5,4},{6,7},{7,6},{8,9},{9,8},{10,11... | collective-permute-start | bytes 786440 | tf_op jit(solution)/shard_map/ppermute | solution.py:76
  109.0 15.6 %collective-permute-start.15 = (bf16[128,1024]{1,0:T(8,128)(2,1)}, bf16[128,1024]{1,0:T(8,128)(2,1)S(1)}, u32[]{:S(2)}, u32[]{:S(2)}) collective-permute-start(bf16[128,1024]{1,0:T(8,128)(2,1)} %get-tuple-element.90), channel_id=1, source_target_pairs={{0,2},{1,3},{2,0},{3,1},{4,6},{5,7},{6,4},{7,5},{8,10},{9,11},{10,... | collective-permute-start | bytes 786440 | tf_op jit(solution)/shard_map/ppermute | solution.py:76
  110.8 13.7 %collective-permute-start.16 = (bf16[128,1024]{1,0:T(8,128)(2,1)}, bf16[128,1024]{1,0:T(8,128)(2,1)S(1)}, u32[]{:S(2)}, u32[]{:S(2)}) collective-permute-start(bf16[128,1024]{1,0:T(8,128)(2,1)} %get-tuple-element.91), channel_id=1, source_target_pairs={{0,3},{1,2},{2,1},{3,0},{4,7},{5,6},{6,5},{7,4},{8,11},{9,10},{10,... | collective-permute-start | bytes 786440 | tf_op jit(solution)/shard_map/ppermute | solution.py:76
  122.6 9.4 %collective-permute-start.10 = (bf16[128,1024]{1,0:T(8,128)(2,1)}, bf16[128,1024]{1,0:T(8,128)(2,1)S(1)}, u32[]{:S(2)}, u32[]{:S(2)}) collective-permute-start(bf16[128,1024]{1,0:T(8,128)(2,1)} %get-tuple-element.84), channel_id=1, source_target_pairs={{0,1},{1,0},{2,3},{3,2},{4,5},{5,4},{6,7},{7,6},{8,9},{9,8},{10,11... | collective-permute-start | bytes 786440 | tf_op jit(solution)/shard_map/ppermute | solution.py:76
  122.7 9.4 %collective-permute-start.11 = (bf16[128,1024]{1,0:T(8,128)(2,1)}, bf16[128,1024]{1,0:T(8,128)(2,1)S(1)}, u32[]{:S(2)}, u32[]{:S(2)}) collective-permute-start(bf16[128,1024]{1,0:T(8,128)(2,1)} %get-tuple-element.85), channel_id=1, source_target_pairs={{0,2},{1,3},{2,0},{3,1},{4,6},{5,7},{6,4},{7,5},{8,10},{9,11},{10,... | collective-permute-start | bytes 786440 | tf_op jit(solution)/shard_map/ppermute | solution.py:76
  124.4 12.4 %collective-permute-start.12 = (bf16[128,1024]{1,0:T(8,128)(2,1)}, bf16[128,1024]{1,0:T(8,128)(2,1)S(1)}, u32[]{:S(2)}, u32[]{:S(2)}) collective-permute-start(bf16[128,1024]{1,0:T(8,128)(2,1)} %get-tuple-element.86), channel_id=1, source_target_pairs={{0,3},{1,2},{2,1},{3,0},{4,7},{5,6},{6,5},{7,4},{8,11},{9,10},{10,... | collective-permute-start | bytes 786440 | tf_op jit(solution)/shard_map/ppermute | solution.py:76
  132.0 4.8 %copy-start.8 = (bf16[128,1024]{1,0:T(8,128)(2,1)}, bf16[128,1024]{1,0:T(8,128)(2,1)S(1)}, u32[]{:S(2)}) copy-start(bf16[128,1024]{1,0:T(8,128)(2,1)S(1)} %collective-permute-done.10.refs_1_) | copy-start | bytes 786436
  132.1 4.7 %copy-start.10 = (bf16[128,1024]{1,0:T(8,128)(2,1)}, bf16[128,1024]{1,0:T(8,128)(2,1)S(1)}, u32[]{:S(2)}) copy-start(bf16[128,1024]{1,0:T(8,128)(2,1)S(1)} %collective-permute-done.11.refs_2_) | copy-start | bytes 786436
  (10 other events, 10.1 us)
